TPU v7x, 32 devices: a whole 2x2x4 slice. The times are simulated.
32 devices in a mesh: seq: 8 (over z, y), mp: 4 (over x, core).
Axes of the slice: x: 2, y: 2, z: 4, core: 2. Of those that a mesh axis runs over, the one named last changes fastest.
Arguments:
- queries: bfloat16 [3072, 2048], P('seq', 'mp'), may hold values from -110 to 110
- self_keys: bfloat16 [3072, 2048], P('seq', 'mp'), may hold values from -6 to 6
- self_values: bfloat16 [3072, 2048], P('seq', 'mp'), may hold values from -6 to 6
- cross_query: bfloat16 [3072, 2048], P('seq', 'mp'), may hold values from -110 to 110
- memory_keys: bfloat16 [64, 128, 2048], P('seq', None, 'mp'), may hold values from -6 to 6
- memory_values: bfloat16 [64, 128, 2048], P('seq', None, 'mp'), may hold values from -6 to 6
- neighbour_owner: int32 [48, 2], P('seq'), may hold values from 0 to 7, all different within a row; in each aligned block of 6 rows (0 to 5, 6 to 11, ...) at most 2 rows name the same one
- neighbour_slot: int32 [48, 2], P('seq'), may hold values from 0 to 7
- out_weight: bfloat16 [2048, 4096], P('mp'), may hold values from -0.125 to 0.125
- cross_weight: bfloat16 [2048, 4096], P('mp'), may hold values from -0.125 to 0.125
Outputs:
- block_out: bfloat16 [3072, 4096], P('seq', 'mp')
Inputs may be any that keep to these rules, and one draw needn't show every extreme that they name: `neighbour_owner`: the 2 neighbours of a span have different owners; among the spans of one index of seq, at most 2 neighbours have one owner.
All inputs are finite; a program needn't handle non-finite values.
Results may differ from a plain program's by a relative error of at most 0.025.
Values may be sent and summed in bfloat16 or wider, within the bound.
A program may use at most 128 MiB of HBM per device.

v0:
```python
import jax
import jax.numpy as jnp
from jax import lax
from jax.sharding import PartitionSpec as P

HEAD = 128
SPAN = 64


NEG_FILL = -1e30


def from_behind(value, axis, steps):
    count = lax.axis_size(axis)
    leading, last = (max(0, -steps), min(count, count - steps))
    return lax.ppermute(value, axis, [(source, source + steps) for source in range(leading, last)])


def split_heads(matrix_block, head_width):
    return matrix_block.reshape(
        matrix_block.shape[:-1] + (matrix_block.shape[-1] // head_width, head_width)
    )


def attend_block(carried, queries, key_value, causal):
    running, totals, numerator = carried
    query_heads = split_heads(queries, HEAD)
    key_heads = split_heads(key_value[0], HEAD)
    value_heads = split_heads(key_value[1], HEAD)
    scores = jnp.einsum(
        "tha,uha->htu", query_heads, key_heads, preferred_element_type=jnp.float32
    ) * HEAD ** (-0.5)
    row_count = queries.shape[0]
    causal_ok = lax.broadcasted_iota(jnp.int32, (row_count, row_count), 0) >= lax.broadcasted_iota(
        jnp.int32, (row_count, row_count), 1
    )
    allowed = jnp.logical_or(causal_ok, jnp.logical_not(causal))
    masked = jnp.where(allowed[None], scores, NEG_FILL)
    newest = jnp.maximum(running, jnp.max(masked, axis=2))
    weights = jnp.exp(masked - newest[..., None])
    factor = jnp.exp(running - newest)
    totals = totals * factor + jnp.sum(weights, axis=2)
    numerator = numerator * factor[..., None] + jnp.einsum(
        "htu,uha->hta",
        weights.astype(jnp.bfloat16),
        value_heads,
        preferred_element_type=jnp.float32,
    )
    return (newest, totals, numerator)


def visit(carried, queries, key_value, source, own_index):
    return lax.cond(
        source < own_index,
        lambda status: attend_block(status, queries, key_value, False),
        lambda status: status,
        carried,
    )


def pass_lower(key_value):
    return from_behind(key_value, "seq", 1)


def self_attention(queries, self_keys, self_values):
    devices = lax.axis_size("seq")
    own_index = lax.axis_index("seq")
    row_count = queries.shape[0]
    heads_here = queries.shape[1] // HEAD
    key_value = jnp.stack([self_keys, self_values])
    initial = (
        jnp.full((heads_here, row_count), NEG_FILL, jnp.float32),
        jnp.zeros((heads_here, row_count), jnp.float32),
        jnp.zeros((heads_here, row_count, HEAD), jnp.float32),
    )
    carried = attend_block(initial, queries, key_value, True)

    def one_way(turn_index, status):
        travel, inner_state = status
        travel = pass_lower(travel)
        return (
            travel,
            visit(inner_state, queries, travel, (own_index - turn_index) % devices, own_index),
        )

    travel, carried = lax.fori_loop(1, devices, one_way, (key_value, carried))
    running, totals, numerator = carried
    blended = numerator / totals[..., None]
    return (
        jnp.transpose(blended, (1, 0, 2)).reshape(row_count, heads_here * HEAD).astype(jnp.bfloat16)
    )


def cross_attention(cross_query, memory_keys, memory_values, neighbour_owner, neighbour_slot):
    devices = lax.axis_size("seq")
    span_count = neighbour_owner.shape[0]
    pick_count = neighbour_owner.shape[1]
    request_count = span_count * pick_count
    capacity = max(2, (request_count + devices - 1) // devices)
    slot_total = devices * capacity
    feature_count = cross_query.shape[1]
    heads_here = feature_count // HEAD
    owner_list = neighbour_owner.reshape(request_count)
    slot_list = neighbour_slot.reshape(request_count)
    owner_hits = (owner_list[:, None] == jnp.arange(devices, dtype=jnp.int32)[None, :]).astype(
        jnp.int32
    )
    earlier = jnp.cumsum(owner_hits, axis=0) - owner_hits
    rank_within = jnp.sum(earlier * owner_hits, axis=1)
    target_slot = owner_list * capacity + rank_within
    routing = target_slot[:, None] == jnp.arange(slot_total, dtype=jnp.int32)[None, :]
    span_rows = cross_query.reshape(span_count, SPAN * feature_count)
    request_rows = jnp.repeat(span_rows, pick_count, axis=0)
    outgoing = jnp.dot(
        jnp.transpose(routing).astype(jnp.bfloat16),
        request_rows,
        preferred_element_type=jnp.float32,
    ).astype(jnp.bfloat16)
    outgoing = outgoing.reshape(devices, capacity, SPAN, feature_count)
    asked_slots = jnp.sum(jnp.where(routing, slot_list[:, None], 0), axis=0).reshape(
        devices, capacity
    )
    asked = lax.all_to_all(outgoing, "seq", split_axis=0, concat_axis=0, tiled=True)
    wanted = lax.all_to_all(asked_slots, "seq", split_axis=0, concat_axis=0, tiled=True)
    source_count = wanted.shape[0]
    item_count = wanted.shape[1]
    key_heads = split_heads(memory_keys[wanted], HEAD)
    value_heads = split_heads(memory_values[wanted], HEAD)
    query_heads = split_heads(asked, HEAD)
    scores = jnp.einsum(
        "nicha,nikha->nihck", query_heads, key_heads, preferred_element_type=jnp.float32
    ) * HEAD ** (-0.5)
    highest = jnp.max(scores, axis=4)
    weights = jnp.exp(scores - highest[..., None])
    totals = jnp.sum(weights, axis=4)
    blended = jnp.einsum(
        "nihck,nikha->nicha",
        weights.astype(jnp.bfloat16),
        value_heads,
        preferred_element_type=jnp.float32,
    )
    blended = blended / jnp.transpose(totals, (0, 1, 3, 2))[..., None]
    answer = blended.reshape(source_count, item_count, SPAN, feature_count).astype(jnp.bfloat16)
    log_mass = highest + jnp.log(totals)
    answers = lax.all_to_all(answer, "seq", split_axis=0, concat_axis=0, tiled=True)
    log_masses = lax.all_to_all(
        log_mass.astype(jnp.bfloat16), "seq", split_axis=0, concat_axis=0, tiled=True
    ).astype(log_mass.dtype)
    answer_rows = jnp.dot(
        routing.astype(jnp.bfloat16),
        answers.reshape(slot_total, SPAN * feature_count),
        preferred_element_type=jnp.float32,
    )
    mass_rows = jnp.dot(
        routing.astype(jnp.float32),
        log_masses.reshape(slot_total, heads_here * SPAN),
        precision=lax.Precision.HIGHEST,
    )
    answer_rows = answer_rows.reshape(span_count, pick_count, SPAN, heads_here, HEAD)
    mass_rows = mass_rows.reshape(span_count, pick_count, heads_here, SPAN)
    best_mass = jnp.max(mass_rows, axis=1, keepdims=True)
    shares = jnp.exp(mass_rows - best_mass)
    share_cols = jnp.transpose(shares, (0, 1, 3, 2))[..., None]
    combined = jnp.sum(share_cols * answer_rows, axis=1) / jnp.sum(share_cols, axis=1)
    return combined.reshape(span_count * SPAN, feature_count).astype(jnp.bfloat16)


def per_device(
    queries,
    self_keys,
    self_values,
    cross_query,
    memory_keys,
    memory_values,
    neighbour_owner,
    neighbour_slot,
    out_weight,
    cross_weight,
):
    attended = self_attention(queries, self_keys, self_values)
    retrieved = cross_attention(
        cross_query, memory_keys, memory_values, neighbour_owner, neighbour_slot
    )
    partial_value = jnp.dot(attended, out_weight, preferred_element_type=jnp.float32)
    partial_value = partial_value + jnp.dot(
        retrieved, cross_weight, preferred_element_type=jnp.float32
    )
    return lax.psum_scatter(
        partial_value.astype(jnp.bfloat16), "mp", scatter_dimension=1, tiled=True
    )


def solution(mesh):
    placed = (
        P("seq", "mp"),
        P("seq", "mp"),
        P("seq", "mp"),
        P("seq", "mp"),
        P("seq", None, "mp"),
        P("seq", None, "mp"),
        P("seq", None),
        P("seq", None),
        P("mp", None),
        P("mp", None),
    )
    return jax.shard_map(
        per_device, mesh=mesh, in_specs=placed, out_specs=P("seq", "mp"), check_vma=False
    )
```

profile of v0, /device:TPU:0, one launch (start us, length us, event | category | flops | bytes accessed | tf_op | source)
XLA Modules:
  0.0 320.3 jit_solution(1754445644933671382)
XLA Ops:
  9.3 7.3 %all-to-all-start.1 = ((s32[8,1,2]{2,1,0:T(1,128)}), s32[8,1,2]{2,1,0:T(1,128)S(1)}, u32[]{:S(2)}, u32[]{:S(2)}) async-start(s32[8,1,2]{2,1,0:T(1,128)} %bitcast.9), calls=%async_computation.1 | async-start | bytes 8192 | tf_op jit(solution)/shard_map/all_to_all | solution.py:124
  23.0 4.2 %all-to-all-start = ((bf16[8,2,64,512]{3,2,1,0:T(8,128)(2,1)}), bf16[8,2,64,512]{3,2,1,0:T(8,128)(2,1)}, u32[]{:S(2)}, u32[]{:S(2)}) async-start(bf16[8,2,64,512]{3,2,1,0:T(8,128)(2,1)} %bitcast.39), calls=%async_computation | async-start | bytes 2097152 | tf_op jit(solution)/shard_map/all_to_all | solution.py:123
  40.0 12.4 %all-to-all-done = bf16[8,2,64,512]{3,2,1,0:T(8,128)(2,1)} async-done(((bf16[8,2,64,512]{3,2,1,0:T(8,128)(2,1)}), bf16[8,2,64,512]{3,2,1,0:T(8,128)(2,1)}, u32[]{:S(2)}, u32[]{:S(2)}) %all-to-all-start) | async-done | bytes 1048608 | tf_op jit(solution)/shard_map/all_to_all | solution.py:123
  52.4 3.6 %multiply_reduce_fusion.2 = (f32[8,2,4,64]{3,2,1,0:T(4,128)S(1)}, f32[8,2,4,64,128]{4,3,2,1,0:T(8,128)S(1)}) fusion(bf16[8,2,128,4,128]{4,3,2,1,0:T(4,128)(2,1)} %reshape.152, bf16[8,2,64,512]{3,2,1,0:T(8,128)(2,1)} %all-to-all-done), kind=kOutput, calls=%fused_computation.28 | convolution fusion | flops 135262208 | bytes 5259264 | tf_op jit(solution)/shard_map/nicha,nikha->nihck/dot_general | solution.py:130
  60.0 3.4 %all-to-all-start.2 = ((bf16[8,2,256]{2,1,0:T(2,128)(2,1)}), bf16[8,2,256]{2,1,0:T(2,128)(2,1)S(1)}, u32[]{:S(2)}, u32[]{:S(2)}) async-start(bf16[8,2,256]{2,1,0:T(2,128)(2,1)} %reshape.180), calls=%async_computation.2 | async-start | bytes 16384 | tf_op jit(solution)/shard_map/all_to_all | solution.py:146
  69.8 4.3 %all-to-all-start.3 = ((bf16[8,2,64,512]{3,2,1,0:T(8,128)(2,1)}), bf16[8,2,64,512]{3,2,1,0:T(8,128)(2,1)}, u32[]{:S(2)}, u32[]{:S(2)}) async-start(bf16[8,2,64,512]{3,2,1,0:T(8,128)(2,1)} %bitcast.118), calls=%async_computation.3 | async-start | bytes 2097152 | tf_op jit(solution)/shard_map/all_to_all | solution.py:145
  77.9 163.0 %while.21 = (s32[]{:T(128)}, bf16[2,384,512]{1,2,0:T(8,128)(2,1)}, f32[4,384]{1,0:T(4,128)S(1)}, f32[4,384]{1,0:T(4,128)S(1)}, f32[4,384,128]{2,1,0:T(8,128)S(1)...) while((s32[]{:T(128)}, bf16[2,384,512]{1,2,0:T(8,128)(2,1)}, ...), condition=%wide.region_7.8_spmd, body=%wide.region_2.7_spmd.sunk | while | flops 307104768 | bytes 16220540 | solution.py:86
  77.9 3.6 %collective-permute-start = (bf16[2,384,512]{1,2,0:T(8,128)(2,1)}, bf16[2,384,512]{1,2,0:T(8,128)(2,1)S(1)}, u32[]{:S(2)}, u32[]{:S(2)}) collective-permute-start(bf16[2,384,512]{1,2,0:T(8,128)(2,1)} %get-tuple-element.321), channel_id=1, source_target_pairs={{0,4},{4,8},{8,12},{12,16},{16,20},{20,24},{24,28},{1,5},{5,9},{9,... | collective-permute-start | bytes 2359304 | tf_op jit(solution)/shard_map/while/body/eval_jaxpr/ppermute | solution.py:16
  81.6 19.9 %collective-permute-done = bf16[2,384,512]{1,2,0:T(8,128)(2,1)S(1)} collective-permute-done((bf16[2,384,512]{1,2,0:T(8,128)(2,1)}, bf16[2,384,512]{1,2,0:T(8,128)(2,1)S(1)}, u32[]{:S(2)}, u32[]{:S(2)}) %collective-permute-start) | collective-permute-done | bytes 786464 | tf_op jit(solution)/shard_map/while/body/eval_jaxpr/ppermute | solution.py:16
  102.3 12.8 %collective-permute-start = (bf16[2,384,512]{1,2,0:T(8,128)(2,1)}, bf16[2,384,512]{1,2,0:T(8,128)(2,1)S(1)}, u32[]{:S(2)}, u32[]{:S(2)}) collective-permute-start(bf16[2,384,512]{1,2,0:T(8,128)(2,1)} %get-tuple-element.321), channel_id=1, source_target_pairs={{0,4},{4,8},{8,12},{12,16},{16,20},{20,24},{24,28},{1,5},{5,9},{9,... | collective-permute-start | bytes 2359304 | tf_op jit(solution)/shard_map/while/body/eval_jaxpr/ppermute | solution.py:16
  115.2 14.9 %collective-permute-done = bf16[2,384,512]{1,2,0:T(8,128)(2,1)S(1)} collective-permute-done((bf16[2,384,512]{1,2,0:T(8,128)(2,1)}, bf16[2,384,512]{1,2,0:T(8,128)(2,1)S(1)}, u32[]{:S(2)}, u32[]{:S(2)}) %collective-permute-start) | collective-permute-done | bytes 786464 | tf_op jit(solution)/shard_map/while/body/eval_jaxpr/ppermute | solution.py:16
  131.0 5.2 %collective-permute-start = (bf16[2,384,512]{1,2,0:T(8,128)(2,1)}, bf16[2,384,512]{1,2,0:T(8,128)(2,1)S(1)}, u32[]{:S(2)}, u32[]{:S(2)}) collective-permute-start(bf16[2,384,512]{1,2,0:T(8,128)(2,1)} %get-tuple-element.321), channel_id=1, source_target_pairs={{0,4},{4,8},{8,12},{12,16},{16,20},{20,24},{24,28},{1,5},{5,9},{9,... | collective-permute-start | bytes 2359304 | tf_op jit(solution)/shard_map/while/body/eval_jaxpr/ppermute | solution.py:16
  136.3 14.0 %collective-permute-done = bf16[2,384,512]{1,2,0:T(8,128)(2,1)S(1)} collective-permute-done((bf16[2,384,512]{1,2,0:T(8,128)(2,1)}, bf16[2,384,512]{1,2,0:T(8,128)(2,1)S(1)}, u32[]{:S(2)}, u32[]{:S(2)}) %collective-permute-start) | collective-permute-done | bytes 786464 | tf_op jit(solution)/shard_map/while/body/eval_jaxpr/ppermute | solution.py:16
  151.1 12.3 %collective-permute-start = (bf16[2,384,512]{1,2,0:T(8,128)(2,1)}, bf16[2,384,512]{1,2,0:T(8,128)(2,1)S(1)}, u32[]{:S(2)}, u32[]{:S(2)}) collective-permute-start(bf16[2,384,512]{1,2,0:T(8,128)(2,1)} %get-tuple-element.321), channel_id=1, source_target_pairs={{0,4},{4,8},{8,12},{12,16},{16,20},{20,24},{24,28},{1,5},{5,9},{9,... | collective-permute-start | bytes 2359304 | tf_op jit(solution)/shard_map/while/body/eval_jaxpr/ppermute | solution.py:16
  163.5 15.4 %collective-permute-done = bf16[2,384,512]{1,2,0:T(8,128)(2,1)S(1)} collective-permute-done((bf16[2,384,512]{1,2,0:T(8,128)(2,1)}, bf16[2,384,512]{1,2,0:T(8,128)(2,1)S(1)}, u32[]{:S(2)}, u32[]{:S(2)}) %collective-permute-start) | collective-permute-done | bytes 786464 | tf_op jit(solution)/shard_map/while/body/eval_jaxpr/ppermute | solution.py:16
  179.8 5.2 %collective-permute-start = (bf16[2,384,512]{1,2,0:T(8,128)(2,1)}, bf16[2,384,512]{1,2,0:T(8,128)(2,1)S(1)}, u32[]{:S(2)}, u32[]{:S(2)}) collective-permute-start(bf16[2,384,512]{1,2,0:T(8,128)(2,1)} %get-tuple-element.321), channel_id=1, source_target_pairs={{0,4},{4,8},{8,12},{12,16},{16,20},{20,24},{24,28},{1,5},{5,9},{9,... | collective-permute-start | bytes 2359304 | tf_op jit(solution)/shard_map/while/body/eval_jaxpr/ppermute | solution.py:16
  185.0 14.5 %collective-permute-done = bf16[2,384,512]{1,2,0:T(8,128)(2,1)S(1)} collective-permute-done((bf16[2,384,512]{1,2,0:T(8,128)(2,1)}, bf16[2,384,512]{1,2,0:T(8,128)(2,1)S(1)}, u32[]{:S(2)}, u32[]{:S(2)}) %collective-permute-start) | collective-permute-done | bytes 786464 | tf_op jit(solution)/shard_map/while/body/eval_jaxpr/ppermute | solution.py:16
  200.4 7.2 %collective-permute-start = (bf16[2,384,512]{1,2,0:T(8,128)(2,1)}, bf16[2,384,512]{1,2,0:T(8,128)(2,1)S(1)}, u32[]{:S(2)}, u32[]{:S(2)}) collective-permute-start(bf16[2,384,512]{1,2,0:T(8,128)(2,1)} %get-tuple-element.321), channel_id=1, source_target_pairs={{0,4},{4,8},{8,12},{12,16},{16,20},{20,24},{24,28},{1,5},{5,9},{9,... | collective-permute-start | bytes 2359304 | tf_op jit(solution)/shard_map/while/body/eval_jaxpr/ppermute | solution.py:16
  207.7 13.6 %collective-permute-done = bf16[2,384,512]{1,2,0:T(8,128)(2,1)S(1)} collective-permute-done((bf16[2,384,512]{1,2,0:T(8,128)(2,1)}, bf16[2,384,512]{1,2,0:T(8,128)(2,1)S(1)}, u32[]{:S(2)}, u32[]{:S(2)}) %collective-permute-start) | collective-permute-done | bytes 786464 | tf_op jit(solution)/shard_map/while/body/eval_jaxpr/ppermute | solution.py:16
  222.2 5.2 %collective-permute-start = (bf16[2,384,512]{1,2,0:T(8,128)(2,1)}, bf16[2,384,512]{1,2,0:T(8,128)(2,1)S(1)}, u32[]{:S(2)}, u32[]{:S(2)}) collective-permute-start(bf16[2,384,512]{1,2,0:T(8,128)(2,1)} %get-tuple-element.321), channel_id=1, source_target_pairs={{0,4},{4,8},{8,12},{12,16},{16,20},{20,24},{24,28},{1,5},{5,9},{9,... | collective-permute-start | bytes 2359304 | tf_op jit(solution)/shard_map/while/body/eval_jaxpr/ppermute | solution.py:16
  227.4 12.7 %collective-permute-done = bf16[2,384,512]{1,2,0:T(8,128)(2,1)S(1)} collective-permute-done((bf16[2,384,512]{1,2,0:T(8,128)(2,1)}, bf16[2,384,512]{1,2,0:T(8,128)(2,1)S(1)}, u32[]{:S(2)}, u32[]{:S(2)}) %collective-permute-start) | collective-permute-done | bytes 786464 | tf_op jit(solution)/shard_map/while/body/eval_jaxpr/ppermute | solution.py:16
  241.3 6.7 %fusion.65 = f32[384,4096]{1,0:T(8,128)} fusion(bf16[384,512]{0,1:T(8,128)(2,1)S(1)} %bitcast.128, bf16[512,4096]{1,0:T(8,128)(2,1)} %param.22), kind=kOutput, calls=%fused_computation.89 | convolution fusion | flops 1610612736 | bytes 10878976 | tf_op jit(solution)/shard_map/dot_general | solution.py:184
  258.2 3.6 %add_convert_fusion = bf16[384,4096]{1,0:T(8,128)(2,1)} fusion(f32[384,4096]{1,0:T(8,128)S(1)} %bitcast.122, bf16[512,4096]{1,0:T(8,128)(2,1)S(1)} %copy-done.2, bf16[48,8,4,128]{3,2,1,0:T(4,128)(2,1)S(1)} %bitcast.125), kind=kOutput, calls=%fused_computation.16 | convolution fusion | flops 1613758464 | bytes 14024704 | tf_op jit(solution)/shard_map/dot_general | solution.py:185
  261.8 51.7 %reduce-scatter.2.cloned.1.call-done = bf16[384,1024]{1,0:T(8,128)(2,1)} async-done(((bf16[384,4096]{1,0:T(8,128)(2,1)}), bf16[384,1024]{1,0:T(8,128)(2,1)}) %reduce-scatter.2.cloned.1.call-update) | async-done | bytes 786448 | tf_op jit(solution)/shard_map/reduce_scatter | solution.py:188
  (113 shorter events, 52.6 us)
Async XLA Ops:
  6.5 26.7 %copy-start = (bf16[8,128,512]{2,1,0:T(8,128)(2,1)S(1)}, bf16[8,128,512]{2,1,0:T(8,128)(2,1)}, u32[]{:S(2)}) copy-start(bf16[8,128,512]{2,1,0:T(8,128)(2,1)} %param.19) | copy-start | bytes 3145732
  9.3 13.7 %all-to-all-start.1 = ((s32[8,1,2]{2,1,0:T(1,128)}), s32[8,1,2]{2,1,0:T(1,128)S(1)}, u32[]{:S(2)}, u32[]{:S(2)}) async-start(s32[8,1,2]{2,1,0:T(1,128)} %bitcast.9), calls=%async_computation.1 | async-start | bytes 8192 | tf_op jit(solution)/shard_map/all_to_all | solution.py:124
  19.3 8.6 %copy-start.8 = (bf16[384,512]{1,0:T(8,128)(2,1)S(1)}, bf16[384,512]{1,0:T(8,128)(2,1)}, u32[]{:S(2)}) copy-start(bf16[384,512]{1,0:T(8,128)(2,1)} %param.15) | copy-start | bytes 1179652
  19.4 9.5 %copy-start.9 = (bf16[384,512]{1,0:T(8,128)(2,1)S(1)}, bf16[384,512]{1,0:T(8,128)(2,1)}, u32[]{:S(2)}) copy-start(bf16[384,512]{1,0:T(8,128)(2,1)} %param.16) | copy-start | bytes 1179652
  20.7 9.1 %copy-start.1 = (bf16[384,512]{1,0:T(8,128)(2,1)S(1)}, bf16[384,512]{1,0:T(8,128)(2,1)}, u32[]{:S(2)}) copy-start(bf16[384,512]{1,0:T(8,128)(2,1)} %param.14) | copy-start | bytes 1179652
  23.0 29.4 %all-to-all-start = ((bf16[8,2,64,512]{3,2,1,0:T(8,128)(2,1)}), bf16[8,2,64,512]{3,2,1,0:T(8,128)(2,1)}, u32[]{:S(2)}, u32[]{:S(2)}) async-start(bf16[8,2,64,512]{3,2,1,0:T(8,128)(2,1)} %bitcast.39), calls=%async_computation | async-start | bytes 2097152 | tf_op jit(solution)/shard_map/all_to_all | solution.py:123
  60.0 9.9 %all-to-all-start.2 = ((bf16[8,2,256]{2,1,0:T(2,128)(2,1)}), bf16[8,2,256]{2,1,0:T(2,128)(2,1)S(1)}, u32[]{:S(2)}, u32[]{:S(2)}) async-start(bf16[8,2,256]{2,1,0:T(2,128)(2,1)} %reshape.180), calls=%async_computation.2 | async-start | bytes 16384 | tf_op jit(solution)/shard_map/all_to_all | solution.py:146
  66.0 8.3 %copy-start.4 = (bf16[384,512]{0,1:T(8,128)(2,1)S(1)}, bf16[384,512]{0,1:T(8,128)(2,1)}, u32[]{:S(2)}) copy-start(bf16[384,512]{0,1:T(8,128)(2,1)} %copy.107) | copy-start | bytes 1179652
  66.0 8.3 %copy-start.5 = (bf16[384,512]{0,1:T(8,128)(2,1)S(1)}, bf16[384,512]{0,1:T(8,128)(2,1)}, u32[]{:S(2)}) copy-start(bf16[384,512]{0,1:T(8,128)(2,1)} %copy.108) | copy-start | bytes 1179652
  67.3 8.1 %copy-start.13 = (f32[4,384]{1,0:T(4,128)S(1)}, f32[4,384]{1,0:T(4,128)}, u32[]{:S(2)}) copy-start(f32[4,384]{1,0:T(4,128)} %fusion.16) | copy-start | bytes 18436
  67.3 8.1 %copy-start.15 = (f32[4,384]{1,0:T(4,128)S(1)}, f32[4,384]{1,0:T(4,128)}, u32[]{:S(2)}) copy-start(f32[4,384]{1,0:T(4,128)} %copy-done.14) | copy-start | bytes 18436
  67.3 8.1 %copy-start.7 = (pred[384,384]{0,1:T(8,128)(4,1)S(1)}, pred[384,384]{0,1:T(8,128)(4,1)}, u32[]{:S(2)}) copy-start(pred[384,384]{0,1:T(8,128)(4,1)} %copy-done.6) | copy-start | bytes 442372
  67.3 8.1 %copy-start.10 = (bf16[384,512]{1,0:T(8,128)(2,1)S(1)}, bf16[384,512]{1,0:T(8,128)(2,1)}, u32[]{:S(2)}) copy-start(bf16[384,512]{1,0:T(8,128)(2,1)} %param.16) | copy-start | bytes 1179652
  69.8 179.0 %all-to-all-start.3 = ((bf16[8,2,64,512]{3,2,1,0:T(8,128)(2,1)}), bf16[8,2,64,512]{3,2,1,0:T(8,128)(2,1)}, u32[]{:S(2)}, u32[]{:S(2)}) async-start(bf16[8,2,64,512]{3,2,1,0:T(8,128)(2,1)} %bitcast.118), calls=%async_computation.3 | async-start | bytes 2097152 | tf_op jit(solution)/shard_map/all_to_all | solution.py:145
  74.1 239.4 %reduce-scatter.2.cloned.1.call-start = ((), (), s32[]{:S(2)}) async-start(), calls=%async_computation.5 | async-start | bytes 3932160 | tf_op jit(solution)/shard_map/reduce_scatter | solution.py:188
  77.9 23.5 %collective-permute-start = (bf16[2,384,512]{1,2,0:T(8,128)(2,1)}, bf16[2,384,512]{1,2,0:T(8,128)(2,1)S(1)}, u32[]{:S(2)}, u32[]{:S(2)}) collective-permute-start(bf16[2,384,512]{1,2,0:T(8,128)(2,1)} %get-tuple-element.321), channel_id=1, source_target_pairs={{0,4},{4,8},{8,12},{12,16},{16,20},{20,24},{24,28},{1,5},{5,9},{9,... | collective-permute-start | bytes 2359304 | tf_op jit(solution)/shard_map/while/body/eval_jaxpr/ppermute | solution.py:16
  102.3 27.8 %collective-permute-start = (bf16[2,384,512]{1,2,0:T(8,128)(2,1)}, bf16[2,384,512]{1,2,0:T(8,128)(2,1)S(1)}, u32[]{:S(2)}, u32[]{:S(2)}) collective-permute-start(bf16[2,384,512]{1,2,0:T(8,128)(2,1)} %get-tuple-element.321), channel_id=1, source_target_pairs={{0,4},{4,8},{8,12},{12,16},{16,20},{20,24},{24,28},{1,5},{5,9},{9,... | collective-permute-start | bytes 2359304 | tf_op jit(solution)/shard_map/while/body/eval_jaxpr/ppermute | solution.py:16
  131.0 19.2 %collective-permute-start = (bf16[2,384,512]{1,2,0:T(8,128)(2,1)}, bf16[2,384,512]{1,2,0:T(8,128)(2,1)S(1)}, u32[]{:S(2)}, u32[]{:S(2)}) collective-permute-start(bf16[2,384,512]{1,2,0:T(8,128)(2,1)} %get-tuple-element.321), channel_id=1, source_target_pairs={{0,4},{4,8},{8,12},{12,16},{16,20},{20,24},{24,28},{1,5},{5,9},{9,... | collective-permute-start | bytes 2359304 | tf_op jit(solution)/shard_map/while/body/eval_jaxpr/ppermute | solution.py:16
  151.1 27.8 %collective-permute-start = (bf16[2,384,512]{1,2,0:T(8,128)(2,1)}, bf16[2,384,512]{1,2,0:T(8,128)(2,1)S(1)}, u32[]{:S(2)}, u32[]{:S(2)}) collective-permute-start(bf16[2,384,512]{1,2,0:T(8,128)(2,1)} %get-tuple-element.321), channel_id=1, source_target_pairs={{0,4},{4,8},{8,12},{12,16},{16,20},{20,24},{24,28},{1,5},{5,9},{9,... | collective-permute-start | bytes 2359304 | tf_op jit(solution)/shard_map/while/body/eval_jaxpr/ppermute | solution.py:16
  179.8 19.8 %collective-permute-start = (bf16[2,384,512]{1,2,0:T(8,128)(2,1)}, bf16[2,384,512]{1,2,0:T(8,128)(2,1)S(1)}, u32[]{:S(2)}, u32[]{:S(2)}) collective-permute-start(bf16[2,384,512]{1,2,0:T(8,128)(2,1)} %get-tuple-element.321), channel_id=1, source_target_pairs={{0,4},{4,8},{8,12},{12,16},{16,20},{20,24},{24,28},{1,5},{5,9},{9,... | collective-permute-start | bytes 2359304 | tf_op jit(solution)/shard_map/while/body/eval_jaxpr/ppermute | solution.py:16
  200.4 20.8 %collective-permute-start = (bf16[2,384,512]{1,2,0:T(8,128)(2,1)}, bf16[2,384,512]{1,2,0:T(8,128)(2,1)S(1)}, u32[]{:S(2)}, u32[]{:S(2)}) collective-permute-start(bf16[2,384,512]{1,2,0:T(8,128)(2,1)} %get-tuple-element.321), channel_id=1, source_target_pairs={{0,4},{4,8},{8,12},{12,16},{16,20},{20,24},{24,28},{1,5},{5,9},{9,... | collective-permute-start | bytes 2359304 | tf_op jit(solution)/shard_map/while/body/eval_jaxpr/ppermute | solution.py:16
  222.2 17.9 %collective-permute-start = (bf16[2,384,512]{1,2,0:T(8,128)(2,1)}, bf16[2,384,512]{1,2,0:T(8,128)(2,1)S(1)}, u32[]{:S(2)}, u32[]{:S(2)}) collective-permute-start(bf16[2,384,512]{1,2,0:T(8,128)(2,1)} %get-tuple-element.321), channel_id=1, source_target_pairs={{0,4},{4,8},{8,12},{12,16},{16,20},{20,24},{24,28},{1,5},{5,9},{9,... | collective-permute-start | bytes 2359304 | tf_op jit(solution)/shard_map/while/body/eval_jaxpr/ppermute | solution.py:16
  241.3 7.0 %copy-start.16 = (s32[6,2]{0,1:T(2,128)S(1)}, s32[6,2]{0,1:T(2,128)}, u32[]{:S(2)}) copy-start(s32[6,2]{0,1:T(2,128)} %copy.116) | copy-start | bytes 148
  251.6 5.8 %slice-start = ((s8[6291456]{0:T(1024)(128)(4,1)}), s8[2097152]{0:T(1024)(128)(4,1)S(1)}, s32[]{:S(2)}) async-start(s8[6291456]{0:T(1024)(128)(4,1)} %bitcast.121), calls=%async_computation.6 | async-start | bytes 4194304
  (7 other events, 16.1 us)
Sparse Core Ops, SparseCore 0:
  261.9 51.5 reduce-scatter.1
where the time goes:
time: 321 us; the launch traced here: 320 us
  waiting for transfers between devices  174 us (54%)
  starting transfers between devices  71 us (22%)
  local copies, waits for them, and re-layouts  33.6 us (10%)
  matrix products  22.9 us (7%)
  between operations  13.7 us (4%)
  other arithmetic  4.82 us (2%)
    ppermute x7, waiting for transfers between devices, from_behind(): lax.ppermute(value, axis, [(source, source + steps) for source in range(l...  105 us
    reduce_scatter x1, waiting for transfers between devices, per_device(): lax.psum_scatter(partial_value.astype(jnp.bfloat16), 'mp', scatter_dimens...  51.7 us
    ppermute x7, starting transfers between devices, from_behind(): lax.ppermute(value, axis, [(source, source + steps) for source in range(l...  51.6 us
    all_to_all x1, waiting for transfers between devices, cross_attention(): lax.all_to_all(outgoing, 'seq', split_axis=0, concat_axis=0, tiled=True)  12.4 us
    unnamed x46, local copies, waits for them, and re-layouts  11.9 us
    all_to_all x1, starting transfers between devices, cross_attention(): lax.all_to_all(asked_slots, 'seq', split_axis=0, concat_axis=0, tiled=True)  7.28 us
    dot_general x1, matrix products, per_device(): jnp.dot(attended, out_weight, preferred_element_type=jnp.float32)  6.69 us
  transfers between devices with their start and end apart: 12, of which 11 were waited for; matrix products, arithmetic and copies ran while one was open for 11% of the time, Pallas kernels for 0%

commit v1 on v0

v1 whole, which is shorter than its diff:
```python
import functools
import math

import jax
import jax.numpy as jnp
from jax import lax
from jax.experimental import pallas as pl
from jax.experimental.pallas import tpu as pltpu
from jax.sharding import PartitionSpec as P

HEAD = 128
SPAN = 64
NEG_FILL = -1e30
SCALE = HEAD ** (-0.5)
LOG2E = math.log2(math.e)
INFO = 16
F32 = jnp.float32
BF16 = jnp.bfloat16


def pack_heads_kernel(q_ref, k_ref, v_ref, out_ref):
    piece = q_ref.shape[0]
    rows = k_ref.shape[0]
    out_ref[0, :piece] = q_ref[...]
    out_ref[0, piece : piece + rows] = k_ref[...]
    out_ref[0, piece + rows :] = v_ref[...]


def pack_heads(queries, self_keys, self_values, devices):
    rows, features = queries.shape
    repeats = devices // (features // HEAD)
    piece = rows // repeats
    whole = pl.BlockSpec((rows, HEAD), lambda d: (0, d // repeats))
    return pl.pallas_call(
        pack_heads_kernel,
        grid=(devices,),
        out_shape=jax.ShapeDtypeStruct((devices, piece + 2 * rows, HEAD), BF16),
        in_specs=[
            pl.BlockSpec((piece, HEAD), lambda d: (d % repeats, d // repeats)),
            whole,
            whole,
        ],
        out_specs=pl.BlockSpec((1, piece + 2 * rows, HEAD), lambda d: (d, 0, 0)),
    )(queries, self_keys, self_values)


def attend_kernel(rows, rep_ref, data_ref, out_ref):
    source = pl.program_id(0)
    piece = out_ref.shape[1]
    query = data_ref[source, :piece]

    def scores_of(j):
        keys = data_ref[j, piece : piece + rows]
        return lax.dot_general(
            query, keys, (((1,), (1,)), ((), ())), preferred_element_type=F32
        ) * (SCALE * LOG2E)

    def mix(j, weights):
        return jnp.dot(
            weights.astype(BF16), data_ref[j, piece + rows :], preferred_element_type=F32
        )

    first = rep_ref[0] * piece
    row_ids = first + lax.broadcasted_iota(jnp.int32, (piece, rows), 0)
    col_ids = lax.broadcasted_iota(jnp.int32, (piece, rows), 1)
    scores = jnp.where(row_ids >= col_ids, scores_of(source), NEG_FILL)
    top = jnp.max(scores, axis=1, keepdims=True)
    weights = jnp.exp2(scores - top)
    total = jnp.sum(weights, axis=1, keepdims=True)
    acc = mix(source, weights)

    def body(j, state):
        top, total, acc = state
        scores = scores_of(j)
        newest = jnp.maximum(top, jnp.max(scores, axis=1, keepdims=True))
        weights = jnp.exp2(scores - newest)
        factor = jnp.exp2(top - newest)
        total = total * factor + jnp.sum(weights, axis=1, keepdims=True)
        return newest, total, acc * factor + mix(j, weights)

    top, total, acc = lax.fori_loop(0, source, body, (top, total, acc))
    out_ref[0] = (acc / total).astype(BF16)


def attend(data, rows):
    devices, height, _ = data.shape
    piece = height - 2 * rows
    heads = devices * piece // rows
    rep = (lax.axis_index("seq") % (rows // piece)).astype(jnp.int32).reshape(1)
    del heads
    return pl.pallas_call(
        functools.partial(attend_kernel, rows),
        grid_spec=pltpu.PrefetchScalarGridSpec(
            num_scalar_prefetch=1,
            grid=(devices,),
            in_specs=[pl.BlockSpec((devices, height, HEAD), lambda s, r: (0, 0, 0))],
            out_specs=pl.BlockSpec((1, piece, HEAD), lambda s, r: (s, 0, 0)),
        ),
        out_shape=jax.ShapeDtypeStruct((devices, piece, HEAD), BF16),
        compiler_params=pltpu.CompilerParams(vmem_limit_bytes=48 * 2**20),
    )(rep, data)


def ask_kernel(capacity, idx_ref, slot_ref, *refs):
    out_ref = refs[-1]
    dest = pl.program_id(0)
    lanes = lax.broadcasted_iota(jnp.int32, (INFO, out_ref.shape[2]), 1)
    info = jnp.zeros(lanes.shape, jnp.int32)
    for item in range(capacity):
        out_ref[0, item * SPAN : (item + 1) * SPAN] = refs[item][...]
        info = jnp.where(lanes == item, slot_ref[dest * capacity + item], info)
    out_ref[0, capacity * SPAN :] = info.astype(F32).astype(BF16)


def ask(cross_query, indices, slots, devices, capacity):
    features = cross_query.shape[1]
    height = capacity * SPAN + INFO
    return pl.pallas_call(
        functools.partial(ask_kernel, capacity),
        grid_spec=pltpu.PrefetchScalarGridSpec(
            num_scalar_prefetch=2,
            grid=(devices,),
            in_specs=[
                pl.BlockSpec(
                    (SPAN, features), lambda d, i, s, item=item: (i[d * capacity + item], 0)
                )
                for item in range(capacity)
            ],
            out_specs=pl.BlockSpec((1, height, features), lambda d, i, s: (d, 0, 0)),
        ),
        out_shape=jax.ShapeDtypeStruct((devices, height, features), BF16),
    )(indices, slots, *([cross_query] * capacity))


def answer_kernel(capacity, want_ref, asked_ref, *refs):
    out_ref = refs[-1]
    features = out_ref.shape[2]
    heads = features // HEAD
    lanes = lax.broadcasted_iota(jnp.int32, (SPAN, HEAD), 1)
    logs = []
    for item in range(capacity):
        keys_ref, values_ref = refs[item], refs[capacity + item]
        rows = slice(item * SPAN, (item + 1) * SPAN)
        info = jnp.zeros((SPAN, HEAD), F32)
        for head in range(heads):
            cols = slice(head * HEAD, (head + 1) * HEAD)
            scores = (
                lax.dot_general(
                    asked_ref[0, rows, cols],
                    keys_ref[0, :, cols],
                    (((1,), (1,)), ((), ())),
                    preferred_element_type=F32,
                )
                * SCALE
            )
            top = jnp.max(scores, axis=1, keepdims=True)
            weights = jnp.exp(scores - top)
            mass = jnp.sum(weights, axis=1, keepdims=True)
            blended = jnp.dot(
                weights.astype(BF16), values_ref[0, :, cols], preferred_element_type=F32
            )
            out_ref[0, rows, cols] = (blended / mass).astype(BF16)
            log_mass = top + jnp.log(mass)
            coarse = log_mass.astype(BF16).astype(F32)
            info = jnp.where(lanes == head, coarse, info)
            info = jnp.where(lanes == heads + head, log_mass - coarse, info)
        logs.append(info)
    turned = jnp.transpose(jnp.concatenate(logs, axis=0))
    out_ref[0, capacity * SPAN :] = jnp.zeros((INFO, features), BF16)
    out_ref[0, capacity * SPAN :, : capacity * SPAN] = turned[:INFO].astype(BF16)


def answer(asked, wanted, memory_keys, memory_values, capacity):
    devices, height, features = asked.shape
    length = memory_keys.shape[1]
    tiles = [
        pl.BlockSpec(
            (1, length, features), lambda s, w, item=item: (w[s * capacity + item], 0, 0)
        )
        for item in range(capacity)
    ]
    block = pl.BlockSpec((1, height, features), lambda s, w: (s, 0, 0))
    return pl.pallas_call(
        functools.partial(answer_kernel, capacity),
        grid_spec=pltpu.PrefetchScalarGridSpec(
            num_scalar_prefetch=1,
            grid=(devices,),
            in_specs=[block] + tiles + tiles,
            out_specs=block,
        ),
        out_shape=jax.ShapeDtypeStruct((devices, height, features), BF16),
    )(wanted, asked, *([memory_keys] * capacity), *([memory_values] * capacity))


def combine_kernel(picks, capacity, owner_ref, rank_ref, *refs):
    out_ref = refs[-1]
    span = pl.program_id(0)
    features = out_ref.shape[1]
    heads = features // HEAD
    starts, logs = [], []
    for n in range(picks):
        rank = rank_ref[span * picks + n]
        starts.append(pl.multiple_of(rank * SPAN, SPAN))
        info = refs[n][0, capacity * SPAN :, : capacity * SPAN].astype(F32)
        turned = jnp.transpose(info)
        chosen = turned[:SPAN]
        for item in range(1, capacity):
            chosen = jnp.where(rank == item, turned[item * SPAN : (item + 1) * SPAN], chosen)
        logs.append(chosen)
    for head in range(heads):
        cols = slice(head * HEAD, (head + 1) * HEAD)
        masses = [c[:, head : head + 1] + c[:, heads + head : heads + head + 1] for c in logs]
        best = functools.reduce(jnp.maximum, masses)
        shares = [jnp.exp(m - best) for m in masses]
        whole = sum(shares)
        mixed = sum(
            share * refs[n][0, pl.ds(starts[n], SPAN), cols].astype(F32)
            for n, share in enumerate(shares)
        )
        out_ref[:, cols] = (mixed / whole).astype(BF16)


def combine(answers, owners, ranks, span_count, picks, capacity):
    devices, height, features = answers.shape
    return pl.pallas_call(
        functools.partial(combine_kernel, picks, capacity),
        grid_spec=pltpu.PrefetchScalarGridSpec(
            num_scalar_prefetch=2,
            grid=(span_count,),
            in_specs=[
                pl.BlockSpec(
                    (1, height, features), lambda c, o, r, n=n: (o[c * picks + n], 0, 0)
                )
                for n in range(picks)
            ],
            out_specs=pl.BlockSpec((SPAN, features), lambda c, o, r: (c, 0)),
        ),
        out_shape=jax.ShapeDtypeStruct((span_count * SPAN, features), BF16),
    )(owners, ranks, *([answers] * picks))


def exchange(value):
    return lax.all_to_all(value, "seq", split_axis=0, concat_axis=0, tiled=True)


def reduce_scatter(partial_value):
    groups = lax.axis_size("mp")
    own = lax.axis_index("mp")
    rows, width = partial_value.shape
    share = width // groups
    blocks = partial_value.reshape(rows, groups // 2, 2, share)
    core = own % 2
    kept = lax.dynamic_index_in_dim(blocks, core, 2, keepdims=False)
    given = lax.dynamic_index_in_dim(blocks, 1 - core, 2, keepdims=False).astype(BF16)
    got = lax.ppermute(given, "mp", [(i, i ^ 1) for i in range(groups)])
    kept = kept + got.astype(F32)
    mine = lax.dynamic_index_in_dim(kept, own // 2, 1, keepdims=False)
    for step in range(1, groups // 2):
        other = lax.dynamic_index_in_dim(kept, (own // 2) ^ step, 1, keepdims=False)
        came = lax.ppermute(
            other.astype(BF16), "mp", [(i, i ^ (2 * step)) for i in range(groups)]
        )
        mine = mine + came.astype(F32)
    return mine.astype(BF16)


def per_device(
    queries,
    self_keys,
    self_values,
    cross_query,
    memory_keys,
    memory_values,
    neighbour_owner,
    neighbour_slot,
    out_weight,
    cross_weight,
):
    devices = lax.axis_size("seq")
    rows, features = queries.shape
    heads = features // HEAD
    span_count, picks = neighbour_owner.shape
    requests = span_count * picks
    capacity = max(2, (requests + devices - 1) // devices)

    owners = neighbour_owner.reshape(requests)
    slots = neighbour_slot.reshape(requests)
    order = jnp.arange(requests, dtype=jnp.int32)
    ranks = jnp.sum(
        ((owners[:, None] == owners[None, :]) & (order[None, :] < order[:, None])).astype(
            jnp.int32
        ),
        axis=1,
    )
    target = owners * capacity + ranks
    hits = target[None, :] == jnp.arange(devices * capacity, dtype=jnp.int32)[:, None]
    indices = jnp.sum(jnp.where(hits, order[None, :] // picks, 0), axis=1)
    sent_slots = jnp.sum(jnp.where(hits, slots[None, :], 0), axis=1)

    asked = exchange(ask(cross_query, indices, sent_slots, devices, capacity))
    data = exchange(pack_heads(queries, self_keys, self_values, devices))
    wanted = asked[:, capacity * SPAN, :capacity].astype(jnp.int32).reshape(devices * capacity)
    answers = exchange(answer(asked, wanted, memory_keys, memory_values, capacity))
    attended = exchange(attend(data, rows))
    retrieved = combine(answers, owners, ranks, span_count, picks, capacity)
    piece = attended.shape[1]
    attended = jnp.transpose(
        attended.reshape(heads, rows // piece, piece, HEAD), (1, 2, 0, 3)
    ).reshape(rows, features)

    partial_value = jnp.dot(attended, out_weight, preferred_element_type=F32)
    partial_value = partial_value + jnp.dot(
        retrieved, cross_weight, preferred_element_type=F32
    )
    return reduce_scatter(partial_value)


def solution(mesh):
    placed = (
        P("seq", "mp"),
        P("seq", "mp"),
        P("seq", "mp"),
        P("seq", "mp"),
        P("seq", None, "mp"),
        P("seq", None, "mp"),
        P("seq", None),
        P("seq", None),
        P("mp", None),
        P("mp", None),
    )
    return jax.shard_map(
        per_device, mesh=mesh, in_specs=placed, out_specs=P("seq", "mp"), check_vma=False
    )
```

time: 321 us -> 214 us (0.67)
  waiting for transfers between devices: 174 us -> 90.4 us
  Pallas kernels: 0 us -> 53.5 us
  starting transfers between devices: 71 us -> 22.1 us
  between operations: 13.7 us -> 0.1 us
  local copies, waits for them, and re-layouts: 33.6 us -> 25.5 us
  matrix products: 22.9 us -> 15.3 us
    ppermute x7 -> x2, waiting for transfers between devices: 105 us -> 18.7 us  [the longest x1 18.7 us: reduce_scatter(): lax.ppermute(other.astype(BF16), 'mp', [(i, i ^ 2 * step) for i in range(...]
    all_to_all x4, waiting for transfers between devices: 17.2 us -> 71.7 us  [exchange(): return lax.all_to_all(value, 'seq', split_axis=0, concat_axis=0, tiled=True)]
    pallas_call x0 -> x5, Pallas kernels: none -> 53.5 us  [the longest x1 19.1 us: answer(): pl.pallas_call(functools.partial(answer_kernel, capacity), grid_spec=pltp...]
    reduce_scatter x1 -> x0, waiting for transfers between devices: 51.7 us -> none  [per_device(): lax.psum_scatter(partial_value.astype(jnp.bfloat16), 'mp', scatter_dimens...]
    ppermute x7 -> x2, starting transfers between devices: 51.6 us -> 1.56 us  [the longest x1 1.49 us: reduce_scatter(): lax.ppermute(other.astype(BF16), 'mp', [(i, i ^ 2 * step) for i in range(...]
    dynamic_slice x0 -> x2, local copies, waits for them, and re-layouts: none -> 12 us  [the longest x1 6.03 us: reduce_scatter(): kept = lax.dynamic_index_in_dim(blocks, core, 2, keepdims=False)]
    unnamed x46 -> x15, local copies, waits for them, and re-layouts: 11.9 us -> 2.13 us
    dot_general x9 -> x2, matrix products: 22.9 us -> 15.3 us  [the longest x1 8.64 us: per_device(): jnp.dot(retrieved, cross_weight, preferred_element_type=F32)]
  transfers between devices with their start and end apart: 12 -> 6, of which waited for: 11 -> 4; matrix products, arithmetic and copies ran while one was open for 11% -> 7% of each run, Pallas kernels for 0% -> 20%
where the time goes in v1:
time: 214 us; the launch traced here: 213 us
  waiting for transfers between devices  90.4 us (42%)
  Pallas kernels  53.5 us (25%)
  local copies, waits for them, and re-layouts  25.5 us (12%)
  starting transfers between devices  22.1 us (10%)
  matrix products  15.3 us (7%)
  other arithmetic  5.6 us (3%)
    all_to_all x4, waiting for transfers between devices, exchange(): return lax.all_to_all(value, 'seq', split_axis=0, concat_axis=0, tiled=True)  71.7 us
    all_to_all x4, starting transfers between devices, exchange(): return lax.all_to_all(value, 'seq', split_axis=0, concat_axis=0, tiled=True)  20.6 us
    pallas_call x1, Pallas kernels, answer(): pl.pallas_call(functools.partial(answer_kernel, capacity), grid_spec=pltp...  19.1 us
    ppermute x1, waiting for transfers between devices, reduce_scatter(): lax.ppermute(other.astype(BF16), 'mp', [(i, i ^ 2 * step) for i in range(...  18.7 us
    pallas_call x1, Pallas kernels, attend(): pl.pallas_call(functools.partial(attend_kernel, rows), grid_spec=pltpu.Pr...  17 us
    reshape x1, local copies, waits for them, and re-layouts, reduce_scatter(): blocks = partial_value.reshape(rows, groups // 2, 2, share)  9.18 us
    dot_general x1, matrix products, per_device(): jnp.dot(retrieved, cross_weight, preferred_element_type=F32)  8.64 us
    dot_general x1, matrix products, per_device(): partial_value = jnp.dot(attended, out_weight, preferred_element_type=F32)  6.66 us
  transfers between devices with their start and end apart: 6, of which 4 were waited for; matrix products, arithmetic and copies ran while one was open for 7% of the time, Pallas kernels for 20%

profile of v1, /device:TPU:0, one launch (start us, length us, event | category | flops | bytes accessed | tf_op | source)
XLA Modules:
  0.0 212.6 jit_solution(4398653290330902586)
XLA Ops:
  0.0 5.6 %shard_map.100 = bf16[8,960,128]{2,1,0:T(8,128)(2,1)} custom-call(bf16[384,512]{1,0:T(8,128)(2,1)} %q_ref.1, bf16[384,512]{1,0:T(8,128)(2,1)} %k_ref.1, bf16[384,512]{1,0:T(8,128)(2,1)} %v_ref.1), custom_call_target="tpu_custom_call" | custom-call | tf_op jit(solution)/shard_map/pallas_call | solution.py:34
  5.6 7.3 %all-to-all-start = ((bf16[8,960,128]{2,1,0:T(8,128)(2,1)}), bf16[8,960,128]{2,1,0:T(8,128)(2,1)S(1)}, u32[]{:S(2)}, u32[]{:S(2)}) async-start(bf16[8,960,128]{2,1,0:T(8,128)(2,1)} %shard_map.100), calls=%async_computation | async-start | bytes 3932160 | tf_op jit(solution)/shard_map/all_to_all | solution.py:243
  14.0 5.7 %shard_map.102 = bf16[8,144,512]{2,1,0:T(8,128)(2,1)} custom-call(s32[16]{0:T(128)} %get-tuple-element.6.idx_ref, s32[16]{0:T(128)} %get-tuple-element.5.slot_ref, bf16[384,512]{1,0:T(8,128)(2,1)} %refs_1_.2, bf16[384,512]{1,0:T(8,128)(2,1)} %refs_1_.2), custom_call_target="tpu_custom_call" | custom-call | tf_op jit(solution)/shard_map/pallas_call | solution.py:118
  19.8 38.5 %all-to-all-done.data_ref = bf16[8,960,128]{2,1,0:T(8,128)(2,1)S(1)} async-done(((bf16[8,960,128]{2,1,0:T(8,128)(2,1)}), bf16[8,960,128]{2,1,0:T(8,128)(2,1)S(1)}, u32[]{:S(2)}, u32[]{:S(2)}) %all-to-all-start) | async-done | bytes 1966112 | tf_op jit(solution)/shard_map/all_to_all | solution.py:243
  58.3 3.6 %all-to-all-start.2 = ((bf16[8,144,512]{2,1,0:T(8,128)(2,1)}), bf16[8,144,512]{2,1,0:T(8,128)(2,1)S(1)}, u32[]{:S(2)}, u32[]{:S(2)}) async-start(bf16[8,144,512]{2,1,0:T(8,128)(2,1)} %shard_map.102), calls=%async_computation.2 | async-start | bytes 2359296 | tf_op jit(solution)/shard_map/all_to_all | solution.py:243
  61.9 17.0 %shard_map.101 = bf16[8,192,128]{2,1,0:T(8,128)(2,1)} custom-call(s32[1]{0:T(128)} %bitcast.rep_ref, bf16[8,960,128]{2,1,0:T(8,128)(2,1)S(1)} %all-to-all-done.data_ref), custom_call_target="tpu_custom_call" | custom-call | tf_op jit(solution)/shard_map/pallas_call | solution.py:91
  78.9 11.8 %all-to-all-done.2.asked_ref = bf16[8,144,512]{2,1,0:T(8,128)(2,1)S(1)} async-done(((bf16[8,144,512]{2,1,0:T(8,128)(2,1)}), bf16[8,144,512]{2,1,0:T(8,128)(2,1)S(1)}, u32[]{:S(2)}, u32[]{:S(2)}) %all-to-all-start.2) | async-done | bytes 1179680 | tf_op jit(solution)/shard_map/all_to_all | solution.py:243
  90.7 3.6 %all-to-all-start.1 = ((bf16[8,192,128]{2,1,0:T(8,128)(2,1)}), bf16[8,192,128]{2,1,0:T(8,128)(2,1)S(1)}, u32[]{:S(2)}, u32[]{:S(2)}) async-start(bf16[8,192,128]{2,1,0:T(8,128)(2,1)} %shard_map.101), calls=%async_computation.1 | async-start | bytes 786432 | tf_op jit(solution)/shard_map/all_to_all | solution.py:243
  95.0 19.1 %shard_map.103 = bf16[8,144,512]{2,1,0:T(8,128)(2,1)} custom-call(s32[16]{0:T(128)} %reshape.74.want_ref, bf16[8,144,512]{2,1,0:T(8,128)(2,1)} %copy-done.1, bf16[8,128,512]{2,1,0:T(8,128)(2,1)} %refs_1_.3, bf16[8,128,512]{2,1,0:T(8,128)(2,1)} %refs_1_.3, bf16[8,128,512]{2,1,0:T(8,128)(2,1)} %refs_3_.1, bf16[8,128,512]{2,1,0:T(8,128)(2,1)} %refs_3_.1), custom_call_target="tpu_custom_call" | custom-call | tf_op jit(solution)/shard_map/pallas_call | solution.py:183
  114.2 6.0 %all-to-all-start.3 = ((bf16[8,144,512]{2,1,0:T(8,128)(2,1)}), bf16[8,144,512]{2,1,0:T(8,128)(2,1)S(1)}, u32[]{:S(2)}, u32[]{:S(2)}) async-start(bf16[8,144,512]{2,1,0:T(8,128)(2,1)} %shard_map.103), calls=%async_computation.3 | async-start | bytes 2359296 | tf_op jit(solution)/shard_map/all_to_all | solution.py:243
  120.5 6.7 %fusion.3 = f32[384,4096]{1,0:T(8,128)} fusion(bf16[512,4096]{1,0:T(8,128)(2,1)} %param.18, bf16[48,8,4,128]{3,2,1,0:T(4,128)(2,1)S(1)} %bitcast.24), kind=kOutput, calls=%fused_computation.8 | convolution fusion | flops 1610612736 | bytes 10878976 | tf_op jit(solution)/shard_map/dot_general | solution.py:311
  127.1 21.3 %all-to-all-done.3.refs_0_.refs_1_ = bf16[8,144,512]{2,1,0:T(8,128)(2,1)S(1)} async-done(((bf16[8,144,512]{2,1,0:T(8,128)(2,1)}), bf16[8,144,512]{2,1,0:T(8,128)(2,1)S(1)}, u32[]{:S(2)}, u32[]{:S(2)}) %all-to-all-start.3) | async-done | bytes 1179680 | tf_op jit(solution)/shard_map/all_to_all | solution.py:243
  148.5 1.1 copy-done
  149.5 6.2 %shard_map.104 = bf16[384,512]{1,0:T(8,128)(2,1)} custom-call(s32[12]{0:T(128)} %copy-done.2, s32[12]{0:T(128)} %copy-done.3, bf16[8,144,512]{2,1,0:T(8,128)(2,1)} %copy-done, bf16[8,144,512]{2,1,0:T(8,128)(2,1)} %copy-done), custom_call_target="tpu_custom_call" | custom-call | tf_op jit(solution)/shard_map/pallas_call | solution.py:225
  155.7 8.6 %convolution_add_fusion = f32[384,4096]{1,0:T(8,128)} fusion(f32[384,4096]{1,0:T(8,128)} %fusion.3, bf16[384,512]{1,0:T(8,128)(2,1)} %shard_map.104, bf16[512,4096]{1,0:T(8,128)(2,1)} %param.19), kind=kOutput, calls=%fused_computation | convolution fusion | flops 1612185600 | bytes 17170432 | tf_op jit(solution)/shard_map/dot_general | solution.py:312
  164.3 9.2 %reshape.73 = f32[384,2,2,1024]{3,2,1,0:T(2,128)} reshape(f32[384,4096]{1,0:T(8,128)} %convolution_add_fusion) | data formatting | bytes 12582912 | tf_op jit(solution)/shard_map/reshape | solution.py:251
  173.5 6.0 %constant_dynamic-slice_fusion = bf16[384,2,1,1024]{3,2,1,0:T(2,128)(2,1)S(1)} fusion(f32[384,2,2,1024]{3,2,1,0:T(2,128)} %reshape.73, s32[]{:T(128)S(6)} %select_n.53), kind=kLoop, calls=%fused_computation.23 | loop fusion | bytes 3145732 | tf_op jit(solution)/shard_map/jit(dynamic_index_in_dim)/dynamic_slice | solution.py:254
  179.5 0.9 copy.35
  180.5 6.0 %constant_dynamic-slice_fusion.1 = f32[384,2,1,1024]{3,2,1,0:T(1,128)S(1)} fusion(f32[384,2,2,1024]{3,2,1,0:T(2,128)} %reshape.73, s32[]{:T(128)S(6)} %select_n.52), kind=kLoop, calls=%fused_computation.24 | loop fusion | bytes 6291460 | tf_op jit(solution)/shard_map/jit(dynamic_index_in_dim)/dynamic_slice | solution.py:253
  186.6 2.5 %bitcast_add_fusion = f32[384,2,1024]{2,0,1:T(8,128)S(1)} fusion(f32[384,2,1,1024]{3,2,1,0:T(1,128)S(1)} %constant_dynamic-slice_fusion.1, bf16[384,2,1024]{2,0,1:T(8,128)(2,1)} %collective-permute-done), kind=kLoop, calls=%fused_computation.2 | loop fusion | flops 1572864 | bytes 7864320 | tf_op jit(solution)/shard_map/add | solution.py:256
  189.0 1.0 fusion.2
  190.1 1.5 collective-permute-start.1
  191.5 18.7 %collective-permute-done.1 = bf16[384,1024]{1,0:T(8,128)(2,1)} collective-permute-done((bf16[384,1024]{1,0:T(8,128)(2,1)}, bf16[384,1024]{1,0:T(8,128)(2,1)}, u32[]{:S(2)}, u32[]{:S(2)}) %collective-permute-start.1) | collective-permute-done | bytes 786464 | tf_op jit(solution)/shard_map/ppermute | solution.py:260
  210.3 2.3 %fusion.1 = bf16[384,1024]{1,0:T(8,128)(2,1)} fusion(bf16[384,1024]{1,0:T(8,128)(2,1)} %collective-permute-done.1, f32[384,2,1024]{2,0,1:T(8,128)S(1)} %bitcast_add_fusion, s32[]{:T(128)S(6)} %select_n.55), kind=kLoop, calls=%fused_computation.5 | loop fusion | flops 1179648 | bytes 3145732 | tf_op jit(solution)/shard_map/convert_element_type | solution.py:264
  (24 shorter events, 2.3 us)
Async XLA Ops:
  0.0 12.9 %copy-start.4 = (s32[6,2]{0,1:T(2,128)S(1)}, s32[6,2]{0,1:T(2,128)}, u32[]{:S(2)}) copy-start(s32[6,2]{0,1:T(2,128)} %param.16) | copy-start | bytes 148
  0.0 13.0 %copy-start.5 = (s32[6,2]{0,1:T(2,128)S(1)}, s32[6,2]{0,1:T(2,128)}, u32[]{:S(2)}) copy-start(s32[6,2]{0,1:T(2,128)} %param.17) | copy-start | bytes 148
  5.6 52.7 %all-to-all-start = ((bf16[8,960,128]{2,1,0:T(8,128)(2,1)}), bf16[8,960,128]{2,1,0:T(8,128)(2,1)S(1)}, u32[]{:S(2)}, u32[]{:S(2)}) async-start(bf16[8,960,128]{2,1,0:T(8,128)(2,1)} %shard_map.100), calls=%async_computation | async-start | bytes 3932160 | tf_op jit(solution)/shard_map/all_to_all | solution.py:243
  13.0 65.8 %copy-start.2 = (s32[12]{0:T(128)}, s32[12]{0:T(128)S(1)}, u32[]{:S(2)}) copy-start(s32[12]{0:T(128)S(1)} %reshape.72.owner_ref) | copy-start | bytes 148
  13.4 65.5 %copy-start.3 = (s32[12]{0:T(128)}, s32[12]{0:T(128)S(1)}, u32[]{:S(2)}) copy-start(s32[12]{0:T(128)S(1)} %convert_reduce_fusion.rank_ref) | copy-start | bytes 148
  58.3 32.4 %all-to-all-start.2 = ((bf16[8,144,512]{2,1,0:T(8,128)(2,1)}), bf16[8,144,512]{2,1,0:T(8,128)(2,1)S(1)}, u32[]{:S(2)}, u32[]{:S(2)}) async-start(bf16[8,144,512]{2,1,0:T(8,128)(2,1)} %shard_map.102), calls=%async_computation.2 | async-start | bytes 2359296 | tf_op jit(solution)/shard_map/all_to_all | solution.py:243
  90.7 4.3 %copy-start.1 = (bf16[8,144,512]{2,1,0:T(8,128)(2,1)}, bf16[8,144,512]{2,1,0:T(8,128)(2,1)S(1)}, u32[]{:S(2)}) copy-start(bf16[8,144,512]{2,1,0:T(8,128)(2,1)S(1)} %all-to-all-done.2.asked_ref) | copy-start | bytes 3538948
  90.7 23.5 %all-to-all-start.1 = ((bf16[8,192,128]{2,1,0:T(8,128)(2,1)}), bf16[8,192,128]{2,1,0:T(8,128)(2,1)S(1)}, u32[]{:S(2)}, u32[]{:S(2)}) async-start(bf16[8,192,128]{2,1,0:T(8,128)(2,1)} %shard_map.101), calls=%async_computation.1 | async-start | bytes 786432 | tf_op jit(solution)/shard_map/all_to_all | solution.py:243
  114.2 34.3 %all-to-all-start.3 = ((bf16[8,144,512]{2,1,0:T(8,128)(2,1)}), bf16[8,144,512]{2,1,0:T(8,128)(2,1)S(1)}, u32[]{:S(2)}, u32[]{:S(2)}) async-start(bf16[8,144,512]{2,1,0:T(8,128)(2,1)} %shard_map.103), calls=%async_computation.3 | async-start | bytes 2359296 | tf_op jit(solution)/shard_map/all_to_all | solution.py:243
  148.5 1.1 copy-start
  180.4 6.1 %collective-permute-start = (bf16[384,2,1024]{2,0,1:T(8,128)(2,1)S(1)}, bf16[384,2,1024]{2,0,1:T(8,128)(2,1)}, u32[]{:S(2)}, u32[]{:S(2)}) collective-permute-start(bf16[384,2,1024]{2,0,1:T(8,128)(2,1)S(1)} %bitcast.23), channel_id=1, source_target_pairs={{0,1},{1,0},{2,3},{3,2},{4,5},{5,4},{6,7},{7,6},{8,9},{9,8},{10,11... | collective-permute-start | bytes 4718600 | tf_op jit(solution)/shard_map/ppermute | solution.py:255
  190.1 20.2 %collective-permute-start.1 = (bf16[384,1024]{1,0:T(8,128)(2,1)}, bf16[384,1024]{1,0:T(8,128)(2,1)}, u32[]{:S(2)}, u32[]{:S(2)}) collective-permute-start(bf16[384,1024]{1,0:T(8,128)(2,1)} %fusion.2), channel_id=1, source_target_pairs={{0,2},{1,3},{2,0},{3,1},{4,6},{5,7},{6,4},{7,5},{8,10},{9,11},{10,... | collective-permute-start | bytes 2359304 | tf_op jit(solution)/shard_map/ppermute | solution.py:260

commit v2 on v1

--- a/solution.py
+++ b/solution.py
@@ -243,25 +243,55 @@
     return lax.all_to_all(value, "seq", split_axis=0, concat_axis=0, tiled=True)
 
 
-def reduce_scatter(partial_value):
+def project_kernel(block_ref, att_ref, ret_ref, out_weight_ref, cross_weight_ref, out_ref):
+    total = jnp.dot(att_ref[...], out_weight_ref[...], preferred_element_type=F32)
+    total += jnp.dot(ret_ref[...], cross_weight_ref[...], preferred_element_type=F32)
+    out_ref[...] = total.astype(BF16)
+
+
+def project(attended, retrieved, out_weight, cross_weight, block, width):
+    rows, features = attended.shape
+    tiles = 2
+    tile = width // tiles
+    left = pl.BlockSpec((rows, features), lambda t, b: (0, 0))
+    right = pl.BlockSpec((features, tile), lambda t, b: (0, b[0] * tiles + t))
+    return pl.pallas_call(
+        project_kernel,
+        grid_spec=pltpu.PrefetchScalarGridSpec(
+            num_scalar_prefetch=1,
+            grid=(tiles,),
+            in_specs=[left, left, right, right],
+            out_specs=pl.BlockSpec((rows, tile), lambda t, b: (0, t)),
+        ),
+        out_shape=jax.ShapeDtypeStruct((rows, width), BF16),
+        cost_estimate=pl.CostEstimate(
+            flops=4 * rows * features * width,
+            bytes_accessed=2 * (2 * features * width + rows * (2 * features + width)),
+            transcendentals=0,
+        ),
+    )(block.astype(jnp.int32).reshape(1), attended, retrieved, out_weight, cross_weight)
+
+
+def project_and_sum(attended, retrieved, out_weight, cross_weight):
     groups = lax.axis_size("mp")
     own = lax.axis_index("mp")
-    rows, width = partial_value.shape
-    share = width // groups
-    blocks = partial_value.reshape(rows, groups // 2, 2, share)
-    core = own % 2
-    kept = lax.dynamic_index_in_dim(blocks, core, 2, keepdims=False)
-    given = lax.dynamic_index_in_dim(blocks, 1 - core, 2, keepdims=False).astype(BF16)
-    got = lax.ppermute(given, "mp", [(i, i ^ 1) for i in range(groups)])
-    kept = kept + got.astype(F32)
-    mine = lax.dynamic_index_in_dim(kept, own // 2, 1, keepdims=False)
-    for step in range(1, groups // 2):
-        other = lax.dynamic_index_in_dim(kept, (own // 2) ^ step, 1, keepdims=False)
-        came = lax.ppermute(
-            other.astype(BF16), "mp", [(i, i ^ (2 * step)) for i in range(groups)]
-        )
-        mine = mine + came.astype(F32)
-    return mine.astype(BF16)
+    share = out_weight.shape[1] // groups
+    core, chip = own % 2, own // 2
+    came = []
+    for step in range(groups // 2 - 1, -1, -1):
+        pair = 2 * (chip ^ step)
+        given = project(attended, retrieved, out_weight, cross_weight, pair + 1 - core, share)
+        got = lax.ppermute(given, "mp", [(i, i ^ 1) for i in range(groups)])
+        kept = project(attended, retrieved, out_weight, cross_weight, pair + core, share)
+        total = kept.astype(F32) + got.astype(F32)
+        if step:
+            total, attended = lax.optimization_barrier((total.astype(BF16), attended))
+            came.append(
+                lax.ppermute(total, "mp", [(i, i ^ (2 * step)) for i in range(groups)])
+            )
+    for other in came:
+        total = total + other.astype(F32)
+    return total.astype(BF16)
 
 
 def per_device(
@@ -298,21 +328,22 @@
     sent_slots = jnp.sum(jnp.where(hits, slots[None, :], 0), axis=1)
 
     asked = exchange(ask(cross_query, indices, sent_slots, devices, capacity))
-    data = exchange(pack_heads(queries, self_keys, self_values, devices))
+    packed = pack_heads(queries, self_keys, self_values, devices)
+    asked, packed = lax.optimization_barrier((asked, packed))
+    data = exchange(packed)
     wanted = asked[:, capacity * SPAN, :capacity].astype(jnp.int32).reshape(devices * capacity)
-    answers = exchange(answer(asked, wanted, memory_keys, memory_values, capacity))
-    attended = exchange(attend(data, rows))
+    answered = answer(asked, wanted, memory_keys, memory_values, capacity)
+    data, answered = lax.optimization_barrier((data, answered))
+    answers = exchange(answered)
+    attended = attend(data, rows)
+    answers, attended = lax.optimization_barrier((answers, attended))
+    attended = exchange(attended)
     retrieved = combine(answers, owners, ranks, span_count, picks, capacity)
     piece = attended.shape[1]
     attended = jnp.transpose(
         attended.reshape(heads, rows // piece, piece, HEAD), (1, 2, 0, 3)
     ).reshape(rows, features)
-
-    partial_value = jnp.dot(attended, out_weight, preferred_element_type=F32)
-    partial_value = partial_value + jnp.dot(
-        retrieved, cross_weight, preferred_element_type=F32
-    )
-    return reduce_scatter(partial_value)
+    return project_and_sum(attended, retrieved, out_weight, cross_weight)
 
 
 def solution(mesh):

time: 214 us -> 178 us (0.83)
  local copies, waits for them, and re-layouts: 25.5 us -> 3.41 us
  matrix products: 15.3 us -> 0 us
  Pallas kernels: 53.5 us -> 67.2 us
  waiting for transfers between devices: 90.4 us -> 80.9 us
    dot_general x2 -> x0, matrix products: 15.3 us -> none  [the longest x1 8.64 us: per_device(): jnp.dot(retrieved, cross_weight, preferred_element_type=F32)]
    pallas_call x0 -> x4, Pallas kernels: none -> 13.6 us  [project(): pl.pallas_call(project_kernel, grid_spec=pltpu.PrefetchScalarGridSpec(num...]
    dynamic_slice x2 -> x0, local copies, waits for them, and re-layouts: 12 us -> none  [the longest x1 6.03 us: reduce_scatter(): kept = lax.dynamic_index_in_dim(blocks, core, 2, keepdims=False)]
    reshape x1 -> x0, local copies, waits for them, and re-layouts: 9.18 us -> none  [reduce_scatter(): blocks = partial_value.reshape(rows, groups // 2, 2, share)]
    all_to_all x4, waiting for transfers between devices: 71.7 us -> 66.4 us  [exchange(): return lax.all_to_all(value, 'seq', split_axis=0, concat_axis=0, tiled=True)]
    ppermute x2 -> x3, waiting for transfers between devices: 18.7 us -> 14.6 us  [the longest x1 14.6 us: project_and_sum(): lax.ppermute(total, 'mp', [(i, i ^ 2 * step) for i in range(groups)])]
    add x1 -> x0, other arithmetic: 2.49 us -> none  [reduce_scatter(): kept = kept + got.astype(F32)]
    all_to_all x4, starting transfers between devices: 20.6 us -> 18.2 us  [exchange(): return lax.all_to_all(value, 'seq', split_axis=0, concat_axis=0, tiled=True)]
  transfers between devices with their start and end apart: 6 -> 7, of which waited for: 4 -> 5; matrix products, arithmetic and copies ran while one was open for 7% -> 0% of each run, Pallas kernels for 20% -> 31%
where the time goes in v2:
time: 178 us; the launch traced here: 177 us
  waiting for transfers between devices  80.9 us (45%)
  Pallas kernels  67.2 us (38%)
  starting transfers between devices  20.2 us (11%)
  other arithmetic  4.78 us (3%)
  local copies, waits for them, and re-layouts  3.41 us (2%)
    all_to_all x4, waiting for transfers between devices, exchange(): return lax.all_to_all(value, 'seq', split_axis=0, concat_axis=0, tiled=True)  66.4 us
    pallas_call x1, Pallas kernels, answer(): pl.pallas_call(functools.partial(answer_kernel, capacity), grid_spec=pltp...  19.1 us
    all_to_all x4, starting transfers between devices, exchange(): return lax.all_to_all(value, 'seq', split_axis=0, concat_axis=0, tiled=True)  18.2 us
    pallas_call x1, Pallas kernels, attend(): pl.pallas_call(functools.partial(attend_kernel, rows), grid_spec=pltpu.Pr...  16.9 us
    ppermute x1, waiting for transfers between devices, project_and_sum(): lax.ppermute(total, 'mp', [(i, i ^ 2 * step) for i in range(groups)])  14.6 us
    pallas_call x4, Pallas kernels, project(): pl.pallas_call(project_kernel, grid_spec=pltpu.PrefetchScalarGridSpec(num...  13.6 us
    pallas_call x1, Pallas kernels, combine(): pl.pallas_call(functools.partial(combine_kernel, picks, capacity), grid_s...  6.15 us
    pallas_call x1, Pallas kernels, ask(): pl.pallas_call(functools.partial(ask_kernel, capacity), grid_spec=pltpu.P...  5.77 us
  transfers between devices with their start and end apart: 7, of which 5 were waited for; matrix products, arithmetic and copies ran while one was open for 0% of the time, Pallas kernels for 31%

profile of v2, /device:TPU:0, one launch (start us, length us, event | category | flops | bytes accessed | tf_op | source)
XLA Modules:
  0.0 176.6 jit_solution(3859381601520298254)
XLA Ops:
  0.0 0.8 copy.17
  1.0 0.8 copy.18
  2.6 5.8 %shard_map.100 = bf16[8,144,512]{2,1,0:T(8,128)(2,1)} custom-call(s32[16]{0:T(128)} %get-tuple-element.22.idx_ref, s32[16]{0:T(128)} %get-tuple-element.21.slot_ref, bf16[384,512]{1,0:T(8,128)(2,1)} %refs_1_.2, bf16[384,512]{1,0:T(8,128)(2,1)} %refs_1_.2), custom_call_target="tpu_custom_call" | custom-call | tf_op jit(solution)/shard_map/pallas_call | solution.py:118
  8.4 7.3 %all-to-all-start = ((bf16[8,144,512]{2,1,0:T(8,128)(2,1)}), bf16[8,144,512]{2,1,0:T(8,128)(2,1)S(1)}, u32[]{:S(2)}, u32[]{:S(2)}) async-start(bf16[8,144,512]{2,1,0:T(8,128)(2,1)} %shard_map.100), calls=%async_computation | async-start | bytes 2359296 | tf_op jit(solution)/shard_map/all_to_all | solution.py:243
  15.7 5.5 %shard_map.101 = bf16[8,960,128]{2,1,0:T(8,128)(2,1)} custom-call(bf16[384,512]{1,0:T(8,128)(2,1)} %q_ref.1, bf16[384,512]{1,0:T(8,128)(2,1)} %k_ref.1, bf16[384,512]{1,0:T(8,128)(2,1)} %v_ref.1), custom_call_target="tpu_custom_call" | custom-call | tf_op jit(solution)/shard_map/pallas_call | solution.py:34
  21.2 23.0 %all-to-all-done.asked_ref = bf16[8,144,512]{2,1,0:T(8,128)(2,1)S(1)} async-done(((bf16[8,144,512]{2,1,0:T(8,128)(2,1)}), bf16[8,144,512]{2,1,0:T(8,128)(2,1)S(1)}, u32[]{:S(2)}, u32[]{:S(2)}) %all-to-all-start) | async-done | bytes 1179680 | tf_op jit(solution)/shard_map/all_to_all | solution.py:243
  44.2 3.6 %all-to-all-start.1 = ((bf16[8,960,128]{2,1,0:T(8,128)(2,1)}), bf16[8,960,128]{2,1,0:T(8,128)(2,1)S(1)}, u32[]{:S(2)}, u32[]{:S(2)}) async-start(bf16[8,960,128]{2,1,0:T(8,128)(2,1)} %shard_map.101), calls=%async_computation.1 | async-start | bytes 3932160 | tf_op jit(solution)/shard_map/all_to_all | solution.py:243
  48.5 19.1 %shard_map.102 = bf16[8,144,512]{2,1,0:T(8,128)(2,1)} custom-call(s32[16]{0:T(128)} %reshape.84.want_ref, bf16[8,144,512]{2,1,0:T(8,128)(2,1)} %copy-done.1, bf16[8,128,512]{2,1,0:T(8,128)(2,1)} %refs_1_.3, bf16[8,128,512]{2,1,0:T(8,128)(2,1)} %refs_1_.3, bf16[8,128,512]{2,1,0:T(8,128)(2,1)} %refs_3_.1, bf16[8,128,512]{2,1,0:T(8,128)(2,1)} %refs_3_.1), custom_call_target="tpu_custom_call" | custom-call | tf_op jit(solution)/shard_map/pallas_call | solution.py:183
  67.7 25.8 %all-to-all-done.1.data_ref = bf16[8,960,128]{2,1,0:T(8,128)(2,1)S(1)} async-done(((bf16[8,960,128]{2,1,0:T(8,128)(2,1)}), bf16[8,960,128]{2,1,0:T(8,128)(2,1)S(1)}, u32[]{:S(2)}, u32[]{:S(2)}) %all-to-all-start.1) | async-done | bytes 1966112 | tf_op jit(solution)/shard_map/all_to_all | solution.py:243
  93.5 3.6 %all-to-all-start.2 = ((bf16[8,144,512]{2,1,0:T(8,128)(2,1)}), bf16[8,144,512]{2,1,0:T(8,128)(2,1)S(1)}, u32[]{:S(2)}, u32[]{:S(2)}) async-start(bf16[8,144,512]{2,1,0:T(8,128)(2,1)} %shard_map.102), calls=%async_computation.2 | async-start | bytes 2359296 | tf_op jit(solution)/shard_map/all_to_all | solution.py:243
  97.1 16.9 %shard_map.103 = bf16[8,192,128]{2,1,0:T(8,128)(2,1)} custom-call(s32[1]{0:T(128)} %bitcast.2.rep_ref, bf16[8,960,128]{2,1,0:T(8,128)(2,1)S(1)} %all-to-all-done.1.data_ref), custom_call_target="tpu_custom_call" | custom-call | tf_op jit(solution)/shard_map/pallas_call | solution.py:91
  114.1 11.8 %all-to-all-done.2.refs_0_.refs_1_ = bf16[8,144,512]{2,1,0:T(8,128)(2,1)S(1)} async-done(((bf16[8,144,512]{2,1,0:T(8,128)(2,1)}), bf16[8,144,512]{2,1,0:T(8,128)(2,1)S(1)}, u32[]{:S(2)}, u32[]{:S(2)}) %all-to-all-start.2) | async-done | bytes 1179680 | tf_op jit(solution)/shard_map/all_to_all | solution.py:243
  125.9 3.6 %all-to-all-start.3 = ((bf16[8,192,128]{2,1,0:T(8,128)(2,1)}), bf16[8,192,128]{2,1,0:T(8,128)(2,1)S(1)}, u32[]{:S(2)}, u32[]{:S(2)}) async-start(bf16[8,192,128]{2,1,0:T(8,128)(2,1)} %shard_map.103), calls=%async_computation.3 | async-start | bytes 786432 | tf_op jit(solution)/shard_map/all_to_all | solution.py:243
  129.5 6.2 %shard_map.104.ret_ref = bf16[384,512]{1,0:T(8,128)(2,1)} custom-call(s32[12]{0:T(128)} %copy-done.2, s32[12]{0:T(128)} %copy-done.3, bf16[8,144,512]{2,1,0:T(8,128)(2,1)} %copy-done, bf16[8,144,512]{2,1,0:T(8,128)(2,1)} %copy-done), custom_call_target="tpu_custom_call" | custom-call | tf_op jit(solution)/shard_map/pallas_call | solution.py:225
  135.7 5.7 %all-to-all-done.3 = bf16[8,192,128]{2,1,0:T(8,128)(2,1)S(1)} async-done(((bf16[8,192,128]{2,1,0:T(8,128)(2,1)}), bf16[8,192,128]{2,1,0:T(8,128)(2,1)S(1)}, u32[]{:S(2)}, u32[]{:S(2)}) %all-to-all-start.3) | async-done | bytes 393248 | tf_op jit(solution)/shard_map/all_to_all | solution.py:243
  141.7 0.8 copy.22
  142.5 3.4 %shard_map.106 = bf16[384,1024]{1,0:T(8,128)(2,1)} custom-call(s32[1]{0:T(128)} %bitcast.5.block_ref, bf16[384,512]{1,0:T(8,128)(2,1)} %bitcast.12, bf16[384,512]{1,0:T(8,128)(2,1)} %shard_map.104.ret_ref, bf16[512,4096]{1,0:T(8,128)(2,1)} %out_weight_ref.7, bf16[512,4096]{1,0:T(8,128)(2,1)} %cross_weight_ref.7), custom_call_target="tpu_custom_call" | custom-call | flops 805306368 | bytes 3670016 | tf_op jit(solution)/shard_map/pallas_call | solution.py:258
  145.9 3.4 %shard_map.105 = bf16[384,1024]{1,0:T(8,128)(2,1)} custom-call(s32[1]{0:T(128)} %bitcast.1.block_ref, bf16[384,512]{1,0:T(8,128)(2,1)} %bitcast.13, bf16[384,512]{1,0:T(8,128)(2,1)} %shard_map.104.ret_ref, bf16[512,4096]{1,0:T(8,128)(2,1)} %out_weight_ref.7, bf16[512,4096]{1,0:T(8,128)(2,1)} %cross_weight_ref.7), custom_call_target="tpu_custom_call" | custom-call | flops 805306368 | bytes 3670016 | tf_op jit(solution)/shard_map/pallas_call | solution.py:258
  149.3 1.4 add_convert_fusion.1
  150.8 3.4 %shard_map.108 = bf16[384,1024]{1,0:T(8,128)(2,1)} custom-call(s32[1]{0:T(128)} %bitcast.6.block_ref, bf16[384,512]{1,0:T(8,128)(2,1)} %bitcast.14, bf16[384,512]{1,0:T(8,128)(2,1)} %shard_map.104.ret_ref, bf16[512,4096]{1,0:T(8,128)(2,1)} %out_weight_ref.7, bf16[512,4096]{1,0:T(8,128)(2,1)} %cross_weight_ref.7), custom_call_target="tpu_custom_call" | custom-call | flops 805306368 | bytes 3670016 | tf_op jit(solution)/shard_map/pallas_call | solution.py:258
  154.7 1.5 collective-permute-start.2
  156.1 3.4 %shard_map.107 = bf16[384,1024]{1,0:T(8,128)(2,1)} custom-call(s32[1]{0:T(128)} %bitcast.block_ref, bf16[384,512]{1,0:T(8,128)(2,1)} %bitcast.15, bf16[384,512]{1,0:T(8,128)(2,1)} %shard_map.104.ret_ref, bf16[512,4096]{1,0:T(8,128)(2,1)} %out_weight_ref.7, bf16[512,4096]{1,0:T(8,128)(2,1)} %cross_weight_ref.7), custom_call_target="tpu_custom_call" | custom-call | flops 805306368 | bytes 3670016 | tf_op jit(solution)/shard_map/pallas_call | solution.py:258
  159.6 14.6 %collective-permute-done.2 = bf16[384,1024]{1,0:T(8,128)(2,1)S(1)} collective-permute-done((bf16[384,1024]{1,0:T(8,128)(2,1)S(1)}, bf16[384,1024]{1,0:T(8,128)(2,1)S(1)}, u32[]{:S(2)}, u32[]{:S(2)}) %collective-permute-start.2) | collective-permute-done | bytes 786464 | tf_op jit(solution)/shard_map/ppermute | solution.py:290
  174.1 2.4 %add_convert_fusion = bf16[384,1024]{1,0:T(8,128)(2,1)} fusion(bf16[384,1024]{1,0:T(8,128)(2,1)S(1)} %collective-permute-done.2, bf16[384,1024]{1,0:T(8,128)(2,1)S(1)} %collective-permute-done.1, bf16[384,1024]{1,0:T(8,128)(2,1)} %shard_map.107), kind=kLoop, calls=%fused_computation | loop fusion | flops 2359296 | bytes 3145728 | tf_op jit(solution)/shard_map/convert_element_type | solution.py:294
  (20 shorter events, 2.5 us)
Async XLA Ops:
  0.8 7.5 %copy-start.2 = (s32[12]{0:T(128)}, s32[12]{0:T(128)S(1)}, u32[]{:S(2)}) copy-start(s32[12]{0:T(128)S(1)} %reshape.78.owner_ref) | copy-start | bytes 148
  1.0 7.3 %copy-start.3 = (s32[12]{0:T(128)}, s32[12]{0:T(128)S(1)}, u32[]{:S(2)}) copy-start(s32[12]{0:T(128)S(1)} %convert_reduce_fusion.rank_ref) | copy-start | bytes 148
  8.4 35.9 %all-to-all-start = ((bf16[8,144,512]{2,1,0:T(8,128)(2,1)}), bf16[8,144,512]{2,1,0:T(8,128)(2,1)S(1)}, u32[]{:S(2)}, u32[]{:S(2)}) async-start(bf16[8,144,512]{2,1,0:T(8,128)(2,1)} %shard_map.100), calls=%async_computation | async-start | bytes 2359296 | tf_op jit(solution)/shard_map/all_to_all | solution.py:243
  44.2 3.6 %copy-start.1 = (bf16[8,144,512]{2,1,0:T(8,128)(2,1)}, bf16[8,144,512]{2,1,0:T(8,128)(2,1)S(1)}, u32[]{:S(2)}) copy-start(bf16[8,144,512]{2,1,0:T(8,128)(2,1)S(1)} %all-to-all-done.asked_ref) | copy-start | bytes 3538948
  44.2 49.2 %all-to-all-start.1 = ((bf16[8,960,128]{2,1,0:T(8,128)(2,1)}), bf16[8,960,128]{2,1,0:T(8,128)(2,1)S(1)}, u32[]{:S(2)}, u32[]{:S(2)}) async-start(bf16[8,960,128]{2,1,0:T(8,128)(2,1)} %shard_map.101), calls=%async_computation.1 | async-start | bytes 3932160 | tf_op jit(solution)/shard_map/all_to_all | solution.py:243
  93.5 32.4 %all-to-all-start.2 = ((bf16[8,144,512]{2,1,0:T(8,128)(2,1)}), bf16[8,144,512]{2,1,0:T(8,128)(2,1)S(1)}, u32[]{:S(2)}, u32[]{:S(2)}) async-start(bf16[8,144,512]{2,1,0:T(8,128)(2,1)} %shard_map.102), calls=%async_computation.2 | async-start | bytes 2359296 | tf_op jit(solution)/shard_map/all_to_all | solution.py:243
  125.9 3.6 %copy-start = (bf16[8,144,512]{2,1,0:T(8,128)(2,1)}, bf16[8,144,512]{2,1,0:T(8,128)(2,1)S(1)}, u32[]{:S(2)}) copy-start(bf16[8,144,512]{2,1,0:T(8,128)(2,1)S(1)} %all-to-all-done.2.refs_0_.refs_1_) | copy-start | bytes 3538948
  125.9 15.5 %all-to-all-start.3 = ((bf16[8,192,128]{2,1,0:T(8,128)(2,1)}), bf16[8,192,128]{2,1,0:T(8,128)(2,1)S(1)}, u32[]{:S(2)}, u32[]{:S(2)}) async-start(bf16[8,192,128]{2,1,0:T(8,128)(2,1)} %shard_map.103), calls=%async_computation.3 | async-start | bytes 786432 | tf_op jit(solution)/shard_map/all_to_all | solution.py:243
  145.9 3.4 %collective-permute-start = (bf16[384,1024]{1,0:T(8,128)(2,1)}, bf16[384,1024]{1,0:T(8,128)(2,1)S(1)}, u32[]{:S(2)}, u32[]{:S(2)}) collective-permute-start(bf16[384,1024]{1,0:T(8,128)(2,1)} %shard_map.106), channel_id=1, source_target_pairs={{0,1},{1,0},{2,3},{3,2},{4,5},{5,4},{6,7},{7,6},{8,9},{9,8},{10,11... | collective-permute-start | bytes 2359304 | tf_op jit(solution)/shard_map/ppermute | solution.py:284
  154.2 5.4 %collective-permute-start.1 = (bf16[384,1024]{1,0:T(8,128)(2,1)}, bf16[384,1024]{1,0:T(8,128)(2,1)S(1)}, u32[]{:S(2)}, u32[]{:S(2)}) collective-permute-start(bf16[384,1024]{1,0:T(8,128)(2,1)} %shard_map.108), channel_id=1, source_target_pairs={{0,1},{1,0},{2,3},{3,2},{4,5},{5,4},{6,7},{7,6},{8,9},{9,8},{10,11... | collective-permute-start | bytes 2359304 | tf_op jit(solution)/shard_map/ppermute | solution.py:284
  154.7 19.5 %collective-permute-start.2 = (bf16[384,1024]{1,0:T(8,128)(2,1)S(1)}, bf16[384,1024]{1,0:T(8,128)(2,1)S(1)}, u32[]{:S(2)}, u32[]{:S(2)}) collective-permute-start(bf16[384,1024]{1,0:T(8,128)(2,1)S(1)} %add_convert_fusion.1), channel_id=1, source_target_pairs={{0,2},{1,3},{2,0},{3,1},{4,6},{5,7},{6,4},{7,5},{8,10},{9,11},{10,... | collective-permute-start | bytes 2359304 | tf_op jit(solution)/shard_map/ppermute | solution.py:290

commit v3 on v2

--- a/solution.py
+++ b/solution.py
@@ -19,86 +19,91 @@
 
 
 def pack_heads_kernel(q_ref, k_ref, v_ref, out_ref):
-    piece = q_ref.shape[0]
-    rows = k_ref.shape[0]
-    out_ref[0, :piece] = q_ref[...]
-    out_ref[0, piece : piece + rows] = k_ref[...]
-    out_ref[0, piece + rows :] = v_ref[...]
+    out_ref[0, 0] = q_ref[...]
+    out_ref[0, 1] = k_ref[...]
+    out_ref[0, 2] = v_ref[...]
 
 
 def pack_heads(queries, self_keys, self_values, devices):
     rows, features = queries.shape
     repeats = devices // (features // HEAD)
     piece = rows // repeats
-    whole = pl.BlockSpec((rows, HEAD), lambda d: (0, d // repeats))
+    part = pl.BlockSpec((piece, HEAD), lambda d: (d % repeats, d // repeats))
     return pl.pallas_call(
         pack_heads_kernel,
         grid=(devices,),
-        out_shape=jax.ShapeDtypeStruct((devices, piece + 2 * rows, HEAD), BF16),
-        in_specs=[
-            pl.BlockSpec((piece, HEAD), lambda d: (d % repeats, d // repeats)),
-            whole,
-            whole,
-        ],
-        out_specs=pl.BlockSpec((1, piece + 2 * rows, HEAD), lambda d: (d, 0, 0)),
+        out_shape=jax.ShapeDtypeStruct((devices, 3, piece, HEAD), BF16),
+        in_specs=[part] * 3,
+        out_specs=pl.BlockSpec((1, 3, piece, HEAD), lambda d: (d, 0, 0, 0)),
     )(queries, self_keys, self_values)
 
 
-def attend_kernel(rows, rep_ref, data_ref, out_ref):
+def attend_kernel(repeats, rep_ref, *refs):
+    out_ref = refs[-1]
     source = pl.program_id(0)
     piece = out_ref.shape[1]
-    query = data_ref[source, :piece]
-
-    def scores_of(j):
-        keys = data_ref[j, piece : piece + rows]
+    query = refs[0][source, 0]
+
+    def scores_of(turn, j):
         return lax.dot_general(
-            query, keys, (((1,), (1,)), ((), ())), preferred_element_type=F32
+            query, refs[turn][j, -2 % refs[turn].shape[1]], (((1,), (1,)), ((), ())), preferred_element_type=F32
         ) * (SCALE * LOG2E)
 
-    def mix(j, weights):
-        return jnp.dot(
-            weights.astype(BF16), data_ref[j, piece + rows :], preferred_element_type=F32
+    def mix(turn, j, weights):
+        return jnp.dot(weights.astype(BF16), refs[turn][j, -1 % refs[turn].shape[1]], preferred_element_type=F32)
+
+    def fold(j, all_scores, state):
+        tops = [jnp.max(scores, axis=1, keepdims=True) for scores in all_scores]
+        newest = functools.reduce(jnp.maximum, tops)
+        if state is not None:
+            newest = jnp.maximum(newest, state[0])
+        weights = [jnp.exp2(scores - newest) for scores in all_scores]
+        total = sum(jnp.sum(part, axis=1, keepdims=True) for part in weights)
+        acc = sum(mix(turn, j, part) for turn, part in enumerate(weights))
+        if state is not None:
+            factor = jnp.exp2(state[0] - newest)
+            total += state[1] * factor
+            acc += state[2] * factor
+        return newest, total, acc
+
+    rep = rep_ref[0]
+    row_ids = lax.broadcasted_iota(jnp.int32, (piece, piece), 0)
+    col_ids = lax.broadcasted_iota(jnp.int32, (piece, piece), 1)
+    diagonal = []
+    for turn in range(repeats):
+        ahead = (rep - lax.rem(rep + repeats - turn, repeats)) * piece
+        diagonal.append(
+            jnp.where(row_ids + ahead >= col_ids, scores_of(turn, source), NEG_FILL)
         )
-
-    first = rep_ref[0] * piece
-    row_ids = first + lax.broadcasted_iota(jnp.int32, (piece, rows), 0)
-    col_ids = lax.broadcasted_iota(jnp.int32, (piece, rows), 1)
-    scores = jnp.where(row_ids >= col_ids, scores_of(source), NEG_FILL)
-    top = jnp.max(scores, axis=1, keepdims=True)
-    weights = jnp.exp2(scores - top)
-    total = jnp.sum(weights, axis=1, keepdims=True)
-    acc = mix(source, weights)
+    state = fold(source, diagonal, None)
 
     def body(j, state):
-        top, total, acc = state
-        scores = scores_of(j)
-        newest = jnp.maximum(top, jnp.max(scores, axis=1, keepdims=True))
-        weights = jnp.exp2(scores - newest)
-        factor = jnp.exp2(top - newest)
-        total = total * factor + jnp.sum(weights, axis=1, keepdims=True)
-        return newest, total, acc * factor + mix(j, weights)
-
-    top, total, acc = lax.fori_loop(0, source, body, (top, total, acc))
+        return fold(j, [scores_of(turn, j) for turn in range(repeats)], state)
+
+    _, total, acc = lax.fori_loop(0, source, body, state)
     out_ref[0] = (acc / total).astype(BF16)
 
 
-def attend(data, rows):
-    devices, height, _ = data.shape
-    piece = height - 2 * rows
-    heads = devices * piece // rows
-    rep = (lax.axis_index("seq") % (rows // piece)).astype(jnp.int32).reshape(1)
-    del heads
-    return pl.pallas_call(
-        functools.partial(attend_kernel, rows),
+def attend(data, repeats):
+    devices, _, piece, _ = data.shape
+    rep = (lax.axis_index("seq") % repeats).astype(jnp.int32).reshape(1)
+    held = [data]
+    for turn in range(1, repeats):
+        pairs = [
+            (i, i // repeats * repeats + (i + turn) % repeats) for i in range(devices)
+        ]
+        held.append(lax.ppermute(data[:, 1:], "seq", pairs))
+    return pl.pallas_call(
+        functools.partial(attend_kernel, repeats),
         grid_spec=pltpu.PrefetchScalarGridSpec(
             num_scalar_prefetch=1,
             grid=(devices,),
-            in_specs=[pl.BlockSpec((devices, height, HEAD), lambda s, r: (0, 0, 0))],
+            in_specs=[pl.BlockSpec(part.shape, lambda s, r: (0, 0, 0, 0)) for part in held],
             out_specs=pl.BlockSpec((1, piece, HEAD), lambda s, r: (s, 0, 0)),
         ),
         out_shape=jax.ShapeDtypeStruct((devices, piece, HEAD), BF16),
         compiler_params=pltpu.CompilerParams(vmem_limit_bytes=48 * 2**20),
-    )(rep, data)
+    )(rep, *held)
 
 
 def ask_kernel(capacity, idx_ref, slot_ref, *refs):
@@ -335,7 +340,7 @@
     answered = answer(asked, wanted, memory_keys, memory_values, capacity)
     data, answered = lax.optimization_barrier((data, answered))
     answers = exchange(answered)
-    attended = attend(data, rows)
+    attended = attend(data, devices // heads)
     answers, attended = lax.optimization_barrier((answers, attended))
     attended = exchange(attended)
     retrieved = combine(answers, owners, ranks, span_count, picks, capacity)

time: 178 us -> 184 us (1.034)
  starting transfers between devices: 20.2 us -> 22.7 us
    ppermute x0 -> x1, waiting for transfers between devices: none -> 29.1 us  [attend(): held.append(lax.ppermute(data[:, 1:], 'seq', pairs))]
    all_to_all x4, waiting for transfers between devices: 66.4 us -> 38.2 us  [exchange(): return lax.all_to_all(value, 'seq', split_axis=0, concat_axis=0, tiled=True)]
    ppermute x0 -> x1, starting transfers between devices: none -> 2.02 us  [attend(): held.append(lax.ppermute(data[:, 1:], 'seq', pairs))]
  transfers between devices with their start and end apart: 7 -> 8, of which waited for: 5 -> 5; matrix products, arithmetic and copies ran while one was open for 0% -> 1% of each run, Pallas kernels for 31% -> 31%
where the time goes in v3:
time: 184 us; the launch traced here: 182 us
  waiting for transfers between devices  82 us (45%)
  Pallas kernels  68.3 us (37%)
  starting transfers between devices  22.7 us (12%)
  other arithmetic  4.79 us (3%)
  local copies, waits for them, and re-layouts  4.36 us (2%)
    all_to_all x4, waiting for transfers between devices, exchange(): return lax.all_to_all(value, 'seq', split_axis=0, concat_axis=0, tiled=True)  38.2 us
    ppermute x1, waiting for transfers between devices, attend(): held.append(lax.ppermute(data[:, 1:], 'seq', pairs))  29.1 us
    pallas_call x1, Pallas kernels, answer(): pl.pallas_call(functools.partial(answer_kernel, capacity), grid_spec=pltp...  19.1 us
    all_to_all x4, starting transfers between devices, exchange(): return lax.all_to_all(value, 'seq', split_axis=0, concat_axis=0, tiled=True)  18.9 us
    pallas_call x1, Pallas kernels, attend(): pl.pallas_call(functools.partial(attend_kernel, repeats), grid_spec=pltpu...  18.6 us
    ppermute x1, waiting for transfers between devices, project_and_sum(): lax.ppermute(total, 'mp', [(i, i ^ 2 * step) for i in range(groups)])  14.7 us
    pallas_call x4, Pallas kernels, project(): pl.pallas_call(project_kernel, grid_spec=pltpu.PrefetchScalarGridSpec(num...  13.6 us
    pallas_call x1, Pallas kernels, combine(): pl.pallas_call(functools.partial(combine_kernel, picks, capacity), grid_s...  6.15 us
  transfers between devices with their start and end apart: 8, of which 5 were waited for; matrix products, arithmetic and copies ran while one was open for 1% of the time, Pallas kernels for 31%

profile of v3, /device:TPU:0, one launch (start us, length us, event | category | flops | bytes accessed | tf_op | source)
XLA Modules:
  0.0 182.2 jit_solution(13723557352620651428)
XLA Ops:
  2.6 5.8 %shard_map.100 = bf16[8,144,512]{2,1,0:T(8,128)(2,1)} custom-call(s32[16]{0:T(128)} %get-tuple-element.22.idx_ref, s32[16]{0:T(128)} %get-tuple-element.21.slot_ref, bf16[384,512]{1,0:T(8,128)(2,1)} %refs_1_.2, bf16[384,512]{1,0:T(8,128)(2,1)} %refs_1_.2), custom_call_target="tpu_custom_call" | custom-call | tf_op jit(solution)/shard_map/pallas_call | solution.py:123
  8.4 7.3 %all-to-all-start = ((bf16[8,144,512]{2,1,0:T(8,128)(2,1)}), bf16[8,144,512]{2,1,0:T(8,128)(2,1)S(1)}, u32[]{:S(2)}, u32[]{:S(2)}) async-start(bf16[8,144,512]{2,1,0:T(8,128)(2,1)} %shard_map.100), calls=%async_computation | async-start | bytes 2359296 | tf_op jit(solution)/shard_map/all_to_all | solution.py:248
  15.7 5.0 %shard_map.101 = bf16[8,3,192,128]{3,2,1,0:T(8,128)(2,1)} custom-call(bf16[384,512]{1,0:T(8,128)(2,1)} %q_ref.1, bf16[384,512]{1,0:T(8,128)(2,1)} %k_ref.1, bf16[384,512]{1,0:T(8,128)(2,1)} %v_ref.1), custom_call_target="tpu_custom_call" | custom-call | tf_op jit(solution)/shard_map/pallas_call | solution.py:32
  20.7 23.6 %all-to-all-done.asked_ref = bf16[8,144,512]{2,1,0:T(8,128)(2,1)S(1)} async-done(((bf16[8,144,512]{2,1,0:T(8,128)(2,1)}), bf16[8,144,512]{2,1,0:T(8,128)(2,1)S(1)}, u32[]{:S(2)}, u32[]{:S(2)}) %all-to-all-start) | async-done | bytes 1179680 | tf_op jit(solution)/shard_map/all_to_all | solution.py:248
  44.2 3.6 %all-to-all-start.1 = ((bf16[8,3,192,128]{3,2,1,0:T(8,128)(2,1)}), bf16[8,3,192,128]{3,2,1,0:T(8,128)(2,1)S(1)}, u32[]{:S(2)}, u32[]{:S(2)}) async-start(bf16[8,3,192,128]{3,2,1,0:T(8,128)(2,1)} %shard_map.101), calls=%async_computation.1 | async-start | bytes 2359296 | tf_op jit(solution)/shard_map/all_to_all | solution.py:248
  48.5 19.1 %shard_map.102 = bf16[8,144,512]{2,1,0:T(8,128)(2,1)} custom-call(s32[16]{0:T(128)} %reshape.84.want_ref, bf16[8,144,512]{2,1,0:T(8,128)(2,1)} %copy-done.1, bf16[8,128,512]{2,1,0:T(8,128)(2,1)} %refs_1_.3, bf16[8,128,512]{2,1,0:T(8,128)(2,1)} %refs_1_.3, bf16[8,128,512]{2,1,0:T(8,128)(2,1)} %refs_3_.1, bf16[8,128,512]{2,1,0:T(8,128)(2,1)} %refs_3_.1), custom_call_target="tpu_custom_call" | custom-call | tf_op jit(solution)/shard_map/pallas_call | solution.py:188
  67.6 9.0 %all-to-all-done.1.refs_0_ = bf16[8,3,192,128]{3,2,1,0:T(8,128)(2,1)S(1)} async-done(((bf16[8,3,192,128]{3,2,1,0:T(8,128)(2,1)}), bf16[8,3,192,128]{3,2,1,0:T(8,128)(2,1)S(1)}, u32[]{:S(2)}, u32[]{:S(2)}) %all-to-all-start.1) | async-done | bytes 1179680 | tf_op jit(solution)/shard_map/all_to_all | solution.py:248
  76.6 3.6 %all-to-all-start.2 = ((bf16[8,144,512]{2,1,0:T(8,128)(2,1)}), bf16[8,144,512]{2,1,0:T(8,128)(2,1)S(1)}, u32[]{:S(2)}, u32[]{:S(2)}) async-start(bf16[8,144,512]{2,1,0:T(8,128)(2,1)} %shard_map.102), calls=%async_computation.2 | async-start | bytes 2359296 | tf_op jit(solution)/shard_map/all_to_all | solution.py:248
  80.3 0.9 slice.7
  81.2 2.0 %collective-permute-start = (bf16[8,2,192,128]{3,2,1,0:T(8,128)(2,1)}, bf16[8,2,192,128]{3,2,1,0:T(8,128)(2,1)S(1)}, u32[]{:S(2)}, u32[]{:S(2)}) collective-permute-start(bf16[8,2,192,128]{3,2,1,0:T(8,128)(2,1)} %slice.7), channel_id=1, source_target_pairs={{0,4},{4,0},{8,12},{12,8},{16,20},{20,16},{24,28},{28,24},{1,5},{5... | collective-permute-start | bytes 2359304 | tf_op jit(solution)/shard_map/ppermute | solution.py:95
  83.2 29.1 %collective-permute-done.refs_1_ = bf16[8,2,192,128]{3,2,1,0:T(8,128)(2,1)S(1)} collective-permute-done((bf16[8,2,192,128]{3,2,1,0:T(8,128)(2,1)}, bf16[8,2,192,128]{3,2,1,0:T(8,128)(2,1)S(1)}, u32[]{:S(2)}, u32[]{:S(2)}) %collective-permute-start) | collective-permute-done | bytes 786464 | tf_op jit(solution)/shard_map/ppermute | solution.py:95
  112.3 18.6 %shard_map.103 = bf16[8,192,128]{2,1,0:T(8,128)(2,1)} custom-call(s32[1]{0:T(128)} %bitcast.2.rep_ref, bf16[8,3,192,128]{3,2,1,0:T(8,128)(2,1)S(1)} %all-to-all-done.1.refs_0_, bf16[8,2,192,128]{3,2,1,0:T(8,128)(2,1)S(1)} %collective-permute-done.refs_1_), custom_call_target="tpu_custom_call" | custom-call | tf_op jit(solution)/shard_map/pallas_call | solution.py:96
  130.9 4.3 %all-to-all-start.3 = ((bf16[8,192,128]{2,1,0:T(8,128)(2,1)}), bf16[8,192,128]{2,1,0:T(8,128)(2,1)S(1)}, u32[]{:S(2)}, u32[]{:S(2)}) async-start(bf16[8,192,128]{2,1,0:T(8,128)(2,1)} %shard_map.103), calls=%async_computation.3 | async-start | bytes 786432 | tf_op jit(solution)/shard_map/all_to_all | solution.py:248
  135.2 6.1 %shard_map.104.ret_ref = bf16[384,512]{1,0:T(8,128)(2,1)} custom-call(s32[12]{0:T(128)} %copy-done.2, s32[12]{0:T(128)} %copy-done.3, bf16[8,144,512]{2,1,0:T(8,128)(2,1)} %copy-done, bf16[8,144,512]{2,1,0:T(8,128)(2,1)} %copy-done), custom_call_target="tpu_custom_call" | custom-call | tf_op jit(solution)/shard_map/pallas_call | solution.py:230
  141.4 5.6 %all-to-all-done.3 = bf16[8,192,128]{2,1,0:T(8,128)(2,1)S(1)} async-done(((bf16[8,192,128]{2,1,0:T(8,128)(2,1)}), bf16[8,192,128]{2,1,0:T(8,128)(2,1)S(1)}, u32[]{:S(2)}, u32[]{:S(2)}) %all-to-all-start.3) | async-done | bytes 393248 | tf_op jit(solution)/shard_map/all_to_all | solution.py:248
  147.3 0.8 copy.22
  148.2 3.4 %shard_map.106 = bf16[384,1024]{1,0:T(8,128)(2,1)} custom-call(s32[1]{0:T(128)} %bitcast.5.block_ref, bf16[384,512]{1,0:T(8,128)(2,1)} %bitcast.12, bf16[384,512]{1,0:T(8,128)(2,1)} %shard_map.104.ret_ref, bf16[512,4096]{1,0:T(8,128)(2,1)} %out_weight_ref.7, bf16[512,4096]{1,0:T(8,128)(2,1)} %cross_weight_ref.7), custom_call_target="tpu_custom_call" | custom-call | flops 805306368 | bytes 3670016 | tf_op jit(solution)/shard_map/pallas_call | solution.py:263
  151.5 3.4 %shard_map.105 = bf16[384,1024]{1,0:T(8,128)(2,1)} custom-call(s32[1]{0:T(128)} %bitcast.1.block_ref, bf16[384,512]{1,0:T(8,128)(2,1)} %bitcast.13, bf16[384,512]{1,0:T(8,128)(2,1)} %shard_map.104.ret_ref, bf16[512,4096]{1,0:T(8,128)(2,1)} %out_weight_ref.7, bf16[512,4096]{1,0:T(8,128)(2,1)} %cross_weight_ref.7), custom_call_target="tpu_custom_call" | custom-call | flops 805306368 | bytes 3670016 | tf_op jit(solution)/shard_map/pallas_call | solution.py:263
  155.0 1.4 add_convert_fusion.1
  156.4 3.4 %shard_map.108 = bf16[384,1024]{1,0:T(8,128)(2,1)} custom-call(s32[1]{0:T(128)} %bitcast.6.block_ref, bf16[384,512]{1,0:T(8,128)(2,1)} %bitcast.14, bf16[384,512]{1,0:T(8,128)(2,1)} %shard_map.104.ret_ref, bf16[512,4096]{1,0:T(8,128)(2,1)} %out_weight_ref.7, bf16[512,4096]{1,0:T(8,128)(2,1)} %cross_weight_ref.7), custom_call_target="tpu_custom_call" | custom-call | flops 805306368 | bytes 3670016 | tf_op jit(solution)/shard_map/pallas_call | solution.py:263
  160.3 1.3 collective-permute-start.3
  161.6 3.4 %shard_map.107 = bf16[384,1024]{1,0:T(8,128)(2,1)} custom-call(s32[1]{0:T(128)} %bitcast.block_ref, bf16[384,512]{1,0:T(8,128)(2,1)} %bitcast.15, bf16[384,512]{1,0:T(8,128)(2,1)} %shard_map.104.ret_ref, bf16[512,4096]{1,0:T(8,128)(2,1)} %out_weight_ref.7, bf16[512,4096]{1,0:T(8,128)(2,1)} %cross_weight_ref.7), custom_call_target="tpu_custom_call" | custom-call | flops 805306368 | bytes 3670016 | tf_op jit(solution)/shard_map/pallas_call | solution.py:263
  165.1 14.7 %collective-permute-done.3 = bf16[384,1024]{1,0:T(8,128)(2,1)S(1)} collective-permute-done((bf16[384,1024]{1,0:T(8,128)(2,1)S(1)}, bf16[384,1024]{1,0:T(8,128)(2,1)S(1)}, u32[]{:S(2)}, u32[]{:S(2)}) %collective-permute-start.3) | collective-permute-done | bytes 786464 | tf_op jit(solution)/shard_map/ppermute | solution.py:295
  179.8 2.4 %add_convert_fusion = bf16[384,1024]{1,0:T(8,128)(2,1)} fusion(bf16[384,1024]{1,0:T(8,128)(2,1)S(1)} %collective-permute-done.3, bf16[384,1024]{1,0:T(8,128)(2,1)S(1)} %collective-permute-done.2, bf16[384,1024]{1,0:T(8,128)(2,1)} %shard_map.107), kind=kLoop, calls=%fused_computation | loop fusion | flops 2359296 | bytes 3145728 | tf_op jit(solution)/shard_map/convert_element_type | solution.py:299
  (23 shorter events, 4.0 us)
Async XLA Ops:
  0.8 7.5 %copy-start.2 = (s32[12]{0:T(128)}, s32[12]{0:T(128)S(1)}, u32[]{:S(2)}) copy-start(s32[12]{0:T(128)S(1)} %reshape.78.owner_ref) | copy-start | bytes 148
  1.0 7.3 %copy-start.3 = (s32[12]{0:T(128)}, s32[12]{0:T(128)S(1)}, u32[]{:S(2)}) copy-start(s32[12]{0:T(128)S(1)} %convert_reduce_fusion.rank_ref) | copy-start | bytes 148
  8.4 35.9 %all-to-all-start = ((bf16[8,144,512]{2,1,0:T(8,128)(2,1)}), bf16[8,144,512]{2,1,0:T(8,128)(2,1)S(1)}, u32[]{:S(2)}, u32[]{:S(2)}) async-start(bf16[8,144,512]{2,1,0:T(8,128)(2,1)} %shard_map.100), calls=%async_computation | async-start | bytes 2359296 | tf_op jit(solution)/shard_map/all_to_all | solution.py:248
  44.2 4.3 %copy-start.1 = (bf16[8,144,512]{2,1,0:T(8,128)(2,1)}, bf16[8,144,512]{2,1,0:T(8,128)(2,1)S(1)}, u32[]{:S(2)}) copy-start(bf16[8,144,512]{2,1,0:T(8,128)(2,1)S(1)} %all-to-all-done.asked_ref) | copy-start | bytes 3538948
  44.2 32.4 %all-to-all-start.1 = ((bf16[8,3,192,128]{3,2,1,0:T(8,128)(2,1)}), bf16[8,3,192,128]{3,2,1,0:T(8,128)(2,1)S(1)}, u32[]{:S(2)}, u32[]{:S(2)}) async-start(bf16[8,3,192,128]{3,2,1,0:T(8,128)(2,1)} %shard_map.101), calls=%async_computation.1 | async-start | bytes 2359296 | tf_op jit(solution)/shard_map/all_to_all | solution.py:248
  76.6 54.3 %all-to-all-start.2 = ((bf16[8,144,512]{2,1,0:T(8,128)(2,1)}), bf16[8,144,512]{2,1,0:T(8,128)(2,1)S(1)}, u32[]{:S(2)}, u32[]{:S(2)}) async-start(bf16[8,144,512]{2,1,0:T(8,128)(2,1)} %shard_map.102), calls=%async_computation.2 | async-start | bytes 2359296 | tf_op jit(solution)/shard_map/all_to_all | solution.py:248
  81.2 31.1 %collective-permute-start = (bf16[8,2,192,128]{3,2,1,0:T(8,128)(2,1)}, bf16[8,2,192,128]{3,2,1,0:T(8,128)(2,1)S(1)}, u32[]{:S(2)}, u32[]{:S(2)}) collective-permute-start(bf16[8,2,192,128]{3,2,1,0:T(8,128)(2,1)} %slice.7), channel_id=1, source_target_pairs={{0,4},{4,0},{8,12},{12,8},{16,20},{20,16},{24,28},{28,24},{1,5},{5... | collective-permute-start | bytes 2359304 | tf_op jit(solution)/shard_map/ppermute | solution.py:95
  130.9 4.3 %copy-start = (bf16[8,144,512]{2,1,0:T(8,128)(2,1)}, bf16[8,144,512]{2,1,0:T(8,128)(2,1)S(1)}, u32[]{:S(2)}) copy-start(bf16[8,144,512]{2,1,0:T(8,128)(2,1)S(1)} %all-to-all-done.2.refs_0_.refs_1_) | copy-start | bytes 3538948
  130.9 16.1 %all-to-all-start.3 = ((bf16[8,192,128]{2,1,0:T(8,128)(2,1)}), bf16[8,192,128]{2,1,0:T(8,128)(2,1)S(1)}, u32[]{:S(2)}, u32[]{:S(2)}) async-start(bf16[8,192,128]{2,1,0:T(8,128)(2,1)} %shard_map.103), calls=%async_computation.3 | async-start | bytes 786432 | tf_op jit(solution)/shard_map/all_to_all | solution.py:248
  151.5 3.4 %collective-permute-start.1 = (bf16[384,1024]{1,0:T(8,128)(2,1)}, bf16[384,1024]{1,0:T(8,128)(2,1)S(1)}, u32[]{:S(2)}, u32[]{:S(2)}) collective-permute-start(bf16[384,1024]{1,0:T(8,128)(2,1)} %shard_map.106), channel_id=1, source_target_pairs={{0,1},{1,0},{2,3},{3,2},{4,5},{5,4},{6,7},{7,6},{8,9},{9,8},{10,11... | collective-permute-start | bytes 2359304 | tf_op jit(solution)/shard_map/ppermute | solution.py:289
  159.8 5.2 %collective-permute-start.2 = (bf16[384,1024]{1,0:T(8,128)(2,1)}, bf16[384,1024]{1,0:T(8,128)(2,1)S(1)}, u32[]{:S(2)}, u32[]{:S(2)}) collective-permute-start(bf16[384,1024]{1,0:T(8,128)(2,1)} %shard_map.108), channel_id=1, source_target_pairs={{0,1},{1,0},{2,3},{3,2},{4,5},{5,4},{6,7},{7,6},{8,9},{9,8},{10,11... | collective-permute-start | bytes 2359304 | tf_op jit(solution)/shard_map/ppermute | solution.py:289
  160.3 19.5 %collective-permute-start.3 = (bf16[384,1024]{1,0:T(8,128)(2,1)S(1)}, bf16[384,1024]{1,0:T(8,128)(2,1)S(1)}, u32[]{:S(2)}, u32[]{:S(2)}) collective-permute-start(bf16[384,1024]{1,0:T(8,128)(2,1)S(1)} %add_convert_fusion.1), channel_id=1, source_target_pairs={{0,2},{1,3},{2,0},{3,1},{4,6},{5,7},{6,4},{7,5},{8,10},{9,11},{10,... | collective-permute-start | bytes 2359304 | tf_op jit(solution)/shard_map/ppermute | solution.py:295

commit v4 on v2

--- a/solution.py
+++ b/solution.py
@@ -101,15 +101,19 @@
     )(rep, data)
 
 
-def ask_kernel(capacity, idx_ref, slot_ref, *refs):
-    out_ref = refs[-1]
-    dest = pl.program_id(0)
+def ask_kernel(capacity, idx_ref, slot_ref, query_ref, out_ref):
     lanes = lax.broadcasted_iota(jnp.int32, (INFO, out_ref.shape[2]), 1)
-    info = jnp.zeros(lanes.shape, jnp.int32)
-    for item in range(capacity):
-        out_ref[0, item * SPAN : (item + 1) * SPAN] = refs[item][...]
-        info = jnp.where(lanes == item, slot_ref[dest * capacity + item], info)
-    out_ref[0, capacity * SPAN :] = info.astype(F32).astype(BF16)
+
+    def body(dest, carry):
+        info = jnp.zeros(lanes.shape, jnp.int32)
+        for item in range(capacity):
+            start = pl.multiple_of(idx_ref[dest * capacity + item] * SPAN, SPAN)
+            out_ref[dest, item * SPAN : (item + 1) * SPAN] = query_ref[pl.ds(start, SPAN)]
+            info = jnp.where(lanes == item, slot_ref[dest * capacity + item], info)
+        out_ref[dest, capacity * SPAN :] = info.astype(F32).astype(BF16)
+        return carry
+
+    lax.fori_loop(0, out_ref.shape[0], body, 0)
 
 
 def ask(cross_query, indices, slots, devices, capacity):
@@ -119,17 +123,13 @@
         functools.partial(ask_kernel, capacity),
         grid_spec=pltpu.PrefetchScalarGridSpec(
             num_scalar_prefetch=2,
-            grid=(devices,),
-            in_specs=[
-                pl.BlockSpec(
-                    (SPAN, features), lambda d, i, s, item=item: (i[d * capacity + item], 0)
-                )
-                for item in range(capacity)
-            ],
-            out_specs=pl.BlockSpec((1, height, features), lambda d, i, s: (d, 0, 0)),
+            grid=(1,),
+            in_specs=[pl.BlockSpec(cross_query.shape, lambda d, i, s: (0, 0))],
+            out_specs=pl.BlockSpec((devices, height, features), lambda d, i, s: (0, 0, 0)),
         ),
         out_shape=jax.ShapeDtypeStruct((devices, height, features), BF16),
-    )(indices, slots, *([cross_query] * capacity))
+        compiler_params=pltpu.CompilerParams(vmem_limit_bytes=32 * 2**20),
+    )(indices, slots, cross_query)
 
 
 def answer_kernel(capacity, want_ref, asked_ref, *refs):

time: 178 us -> 174 us (0.978)
  Pallas kernels: 67.2 us -> 63.1 us
    pallas_call x1, Pallas kernels: 5.77 us -> 1.71 us  [ask(): pl.pallas_call(functools.partial(ask_kernel, capacity), grid_spec=pltpu.P...]
  transfers between devices with their start and end apart: 7 -> 7, of which waited for: 5 -> 5; matrix products, arithmetic and copies ran while one was open for 0% -> 0% of each run, Pallas kernels for 31% -> 32%
where the time goes in v4:
time: 174 us; the launch traced here: 173 us
  waiting for transfers between devices  81 us (47%)
  Pallas kernels  63.1 us (36%)
  starting transfers between devices  20.2 us (12%)
  local copies, waits for them, and re-layouts  4.42 us (3%)
  other arithmetic  4.19 us (2%)
    all_to_all x4, waiting for transfers between devices, exchange(): return lax.all_to_all(value, 'seq', split_axis=0, concat_axis=0, tiled=True)  66.4 us
    pallas_call x1, Pallas kernels, answer(): pl.pallas_call(functools.partial(answer_kernel, capacity), grid_spec=pltp...  19.1 us
    all_to_all x4, starting transfers between devices, exchange(): return lax.all_to_all(value, 'seq', split_axis=0, concat_axis=0, tiled=True)  18.2 us
    pallas_call x1, Pallas kernels, attend(): pl.pallas_call(functools.partial(attend_kernel, rows), grid_spec=pltpu.Pr...  16.9 us
    ppermute x1, waiting for transfers between devices, project_and_sum(): lax.ppermute(total, 'mp', [(i, i ^ 2 * step) for i in range(groups)])  14.6 us
    pallas_call x4, Pallas kernels, project(): pl.pallas_call(project_kernel, grid_spec=pltpu.PrefetchScalarGridSpec(num...  13.6 us
    pallas_call x1, Pallas kernels, combine(): pl.pallas_call(functools.partial(combine_kernel, picks, capacity), grid_s...  6.12 us
    pallas_call x1, Pallas kernels, pack_heads(): pl.pallas_call(pack_heads_kernel, grid=(devices,), out_shape=jax.ShapeDty...  5.56 us
  transfers between devices with their start and end apart: 7, of which 5 were waited for; matrix products, arithmetic and copies ran while one was open for 0% of the time, Pallas kernels for 32%

profile of v4, /device:TPU:0, one launch (start us, length us, event | category | flops | bytes accessed | tf_op | source)
XLA Modules:
  0.0 172.9 jit_solution(11641217198190675933)
XLA Ops:
  1.0 0.8 copy.18
  2.0 1.0 copy-done
  3.0 1.7 shard_map.100
  4.7 7.3 %all-to-all-start = ((bf16[8,144,512]{2,1,0:T(8,128)(2,1)}), bf16[8,144,512]{2,1,0:T(8,128)(2,1)S(1)}, u32[]{:S(2)}, u32[]{:S(2)}) async-start(bf16[8,144,512]{2,1,0:T(8,128)(2,1)} %shard_map.100), calls=%async_computation | async-start | bytes 2359296 | tf_op jit(solution)/shard_map/all_to_all | solution.py:243
  12.0 5.6 %shard_map.101 = bf16[8,960,128]{2,1,0:T(8,128)(2,1)} custom-call(bf16[384,512]{1,0:T(8,128)(2,1)} %q_ref.1, bf16[384,512]{1,0:T(8,128)(2,1)} %k_ref.1, bf16[384,512]{1,0:T(8,128)(2,1)} %v_ref.1), custom_call_target="tpu_custom_call" | custom-call | tf_op jit(solution)/shard_map/pallas_call | solution.py:34
  17.6 23.0 %all-to-all-done.asked_ref = bf16[8,144,512]{2,1,0:T(8,128)(2,1)S(1)} async-done(((bf16[8,144,512]{2,1,0:T(8,128)(2,1)}), bf16[8,144,512]{2,1,0:T(8,128)(2,1)S(1)}, u32[]{:S(2)}, u32[]{:S(2)}) %all-to-all-start) | async-done | bytes 1179680 | tf_op jit(solution)/shard_map/all_to_all | solution.py:243
  40.6 3.6 %all-to-all-start.1 = ((bf16[8,960,128]{2,1,0:T(8,128)(2,1)}), bf16[8,960,128]{2,1,0:T(8,128)(2,1)S(1)}, u32[]{:S(2)}, u32[]{:S(2)}) async-start(bf16[8,960,128]{2,1,0:T(8,128)(2,1)} %shard_map.101), calls=%async_computation.1 | async-start | bytes 3932160 | tf_op jit(solution)/shard_map/all_to_all | solution.py:243
  44.9 19.1 %shard_map.102 = bf16[8,144,512]{2,1,0:T(8,128)(2,1)} custom-call(s32[16]{0:T(128)} %reshape.84.want_ref, bf16[8,144,512]{2,1,0:T(8,128)(2,1)} %copy-done.2, bf16[8,128,512]{2,1,0:T(8,128)(2,1)} %refs_1_.1, bf16[8,128,512]{2,1,0:T(8,128)(2,1)} %refs_1_.1, bf16[8,128,512]{2,1,0:T(8,128)(2,1)} %refs_3_.1, bf16[8,128,512]{2,1,0:T(8,128)(2,1)} %refs_3_.1), custom_call_target="tpu_custom_call" | custom-call | tf_op jit(solution)/shard_map/pallas_call | solution.py:183
  64.0 25.8 %all-to-all-done.1.data_ref = bf16[8,960,128]{2,1,0:T(8,128)(2,1)S(1)} async-done(((bf16[8,960,128]{2,1,0:T(8,128)(2,1)}), bf16[8,960,128]{2,1,0:T(8,128)(2,1)S(1)}, u32[]{:S(2)}, u32[]{:S(2)}) %all-to-all-start.1) | async-done | bytes 1966112 | tf_op jit(solution)/shard_map/all_to_all | solution.py:243
  89.8 3.6 %all-to-all-start.2 = ((bf16[8,144,512]{2,1,0:T(8,128)(2,1)}), bf16[8,144,512]{2,1,0:T(8,128)(2,1)S(1)}, u32[]{:S(2)}, u32[]{:S(2)}) async-start(bf16[8,144,512]{2,1,0:T(8,128)(2,1)} %shard_map.102), calls=%async_computation.2 | async-start | bytes 2359296 | tf_op jit(solution)/shard_map/all_to_all | solution.py:243
  93.5 16.9 %shard_map.103 = bf16[8,192,128]{2,1,0:T(8,128)(2,1)} custom-call(s32[1]{0:T(128)} %bitcast.2.rep_ref, bf16[8,960,128]{2,1,0:T(8,128)(2,1)S(1)} %all-to-all-done.1.data_ref), custom_call_target="tpu_custom_call" | custom-call | tf_op jit(solution)/shard_map/pallas_call | solution.py:91
  110.4 11.8 %all-to-all-done.2.refs_0_.refs_1_ = bf16[8,144,512]{2,1,0:T(8,128)(2,1)S(1)} async-done(((bf16[8,144,512]{2,1,0:T(8,128)(2,1)}), bf16[8,144,512]{2,1,0:T(8,128)(2,1)S(1)}, u32[]{:S(2)}, u32[]{:S(2)}) %all-to-all-start.2) | async-done | bytes 1179680 | tf_op jit(solution)/shard_map/all_to_all | solution.py:243
  122.2 3.6 %all-to-all-start.3 = ((bf16[8,192,128]{2,1,0:T(8,128)(2,1)}), bf16[8,192,128]{2,1,0:T(8,128)(2,1)S(1)}, u32[]{:S(2)}, u32[]{:S(2)}) async-start(bf16[8,192,128]{2,1,0:T(8,128)(2,1)} %shard_map.103), calls=%async_computation.3 | async-start | bytes 786432 | tf_op jit(solution)/shard_map/all_to_all | solution.py:243
  125.9 6.1 %shard_map.104.ret_ref = bf16[384,512]{1,0:T(8,128)(2,1)} custom-call(s32[12]{0:T(128)} %copy-done.3, s32[12]{0:T(128)} %copy-done.4, bf16[8,144,512]{2,1,0:T(8,128)(2,1)} %copy-done.1, bf16[8,144,512]{2,1,0:T(8,128)(2,1)} %copy-done.1), custom_call_target="tpu_custom_call" | custom-call | tf_op jit(solution)/shard_map/pallas_call | solution.py:225
  132.0 5.7 %all-to-all-done.3 = bf16[8,192,128]{2,1,0:T(8,128)(2,1)S(1)} async-done(((bf16[8,192,128]{2,1,0:T(8,128)(2,1)}), bf16[8,192,128]{2,1,0:T(8,128)(2,1)S(1)}, u32[]{:S(2)}, u32[]{:S(2)}) %all-to-all-start.3) | async-done | bytes 393248 | tf_op jit(solution)/shard_map/all_to_all | solution.py:243
  138.0 0.8 copy.22
  138.9 3.4 %shard_map.106 = bf16[384,1024]{1,0:T(8,128)(2,1)} custom-call(s32[1]{0:T(128)} %bitcast.5.block_ref, bf16[384,512]{1,0:T(8,128)(2,1)} %bitcast.12, bf16[384,512]{1,0:T(8,128)(2,1)} %shard_map.104.ret_ref, bf16[512,4096]{1,0:T(8,128)(2,1)} %out_weight_ref.7, bf16[512,4096]{1,0:T(8,128)(2,1)} %cross_weight_ref.7), custom_call_target="tpu_custom_call" | custom-call | flops 805306368 | bytes 3670016 | tf_op jit(solution)/shard_map/pallas_call | solution.py:258
  142.2 3.4 %shard_map.105 = bf16[384,1024]{1,0:T(8,128)(2,1)} custom-call(s32[1]{0:T(128)} %bitcast.1.block_ref, bf16[384,512]{1,0:T(8,128)(2,1)} %bitcast.13, bf16[384,512]{1,0:T(8,128)(2,1)} %shard_map.104.ret_ref, bf16[512,4096]{1,0:T(8,128)(2,1)} %out_weight_ref.7, bf16[512,4096]{1,0:T(8,128)(2,1)} %cross_weight_ref.7), custom_call_target="tpu_custom_call" | custom-call | flops 805306368 | bytes 3670016 | tf_op jit(solution)/shard_map/pallas_call | solution.py:258
  145.7 1.4 add_convert_fusion.1
  147.1 3.4 %shard_map.108 = bf16[384,1024]{1,0:T(8,128)(2,1)} custom-call(s32[1]{0:T(128)} %bitcast.6.block_ref, bf16[384,512]{1,0:T(8,128)(2,1)} %bitcast.14, bf16[384,512]{1,0:T(8,128)(2,1)} %shard_map.104.ret_ref, bf16[512,4096]{1,0:T(8,128)(2,1)} %out_weight_ref.7, bf16[512,4096]{1,0:T(8,128)(2,1)} %cross_weight_ref.7), custom_call_target="tpu_custom_call" | custom-call | flops 805306368 | bytes 3670016 | tf_op jit(solution)/shard_map/pallas_call | solution.py:258
  151.0 1.5 collective-permute-start.2
  152.5 3.4 %shard_map.107 = bf16[384,1024]{1,0:T(8,128)(2,1)} custom-call(s32[1]{0:T(128)} %bitcast.block_ref, bf16[384,512]{1,0:T(8,128)(2,1)} %bitcast.15, bf16[384,512]{1,0:T(8,128)(2,1)} %shard_map.104.ret_ref, bf16[512,4096]{1,0:T(8,128)(2,1)} %out_weight_ref.7, bf16[512,4096]{1,0:T(8,128)(2,1)} %cross_weight_ref.7), custom_call_target="tpu_custom_call" | custom-call | flops 805306368 | bytes 3670016 | tf_op jit(solution)/shard_map/pallas_call | solution.py:258
  155.9 14.6 %collective-permute-done.2 = bf16[384,1024]{1,0:T(8,128)(2,1)S(1)} collective-permute-done((bf16[384,1024]{1,0:T(8,128)(2,1)S(1)}, bf16[384,1024]{1,0:T(8,128)(2,1)S(1)}, u32[]{:S(2)}, u32[]{:S(2)}) %collective-permute-start.2) | collective-permute-done | bytes 786464 | tf_op jit(solution)/shard_map/ppermute | solution.py:290
  170.5 2.4 %add_convert_fusion = bf16[384,1024]{1,0:T(8,128)(2,1)} fusion(bf16[384,1024]{1,0:T(8,128)(2,1)S(1)} %collective-permute-done.2, bf16[384,1024]{1,0:T(8,128)(2,1)S(1)} %collective-permute-done.1, bf16[384,1024]{1,0:T(8,128)(2,1)} %shard_map.107), kind=kLoop, calls=%fused_computation | loop fusion | flops 2359296 | bytes 3145728 | tf_op jit(solution)/shard_map/convert_element_type | solution.py:294
  (22 shorter events, 2.7 us)
Async XLA Ops:
  0.8 3.9 %copy-start.3 = (s32[12]{0:T(128)}, s32[12]{0:T(128)S(1)}, u32[]{:S(2)}) copy-start(s32[12]{0:T(128)S(1)} %reshape.78.owner_ref) | copy-start | bytes 148
  1.0 3.7 %copy-start.4 = (s32[12]{0:T(128)}, s32[12]{0:T(128)S(1)}, u32[]{:S(2)}) copy-start(s32[12]{0:T(128)S(1)} %convert_reduce_fusion.rank_ref) | copy-start | bytes 148
  2.0 1.0 copy-start
  4.7 35.9 %all-to-all-start = ((bf16[8,144,512]{2,1,0:T(8,128)(2,1)}), bf16[8,144,512]{2,1,0:T(8,128)(2,1)S(1)}, u32[]{:S(2)}, u32[]{:S(2)}) async-start(bf16[8,144,512]{2,1,0:T(8,128)(2,1)} %shard_map.100), calls=%async_computation | async-start | bytes 2359296 | tf_op jit(solution)/shard_map/all_to_all | solution.py:243
  40.6 3.6 %copy-start.2 = (bf16[8,144,512]{2,1,0:T(8,128)(2,1)}, bf16[8,144,512]{2,1,0:T(8,128)(2,1)S(1)}, u32[]{:S(2)}) copy-start(bf16[8,144,512]{2,1,0:T(8,128)(2,1)S(1)} %all-to-all-done.asked_ref) | copy-start | bytes 3538948
  40.6 49.2 %all-to-all-start.1 = ((bf16[8,960,128]{2,1,0:T(8,128)(2,1)}), bf16[8,960,128]{2,1,0:T(8,128)(2,1)S(1)}, u32[]{:S(2)}, u32[]{:S(2)}) async-start(bf16[8,960,128]{2,1,0:T(8,128)(2,1)} %shard_map.101), calls=%async_computation.1 | async-start | bytes 3932160 | tf_op jit(solution)/shard_map/all_to_all | solution.py:243
  89.8 32.4 %all-to-all-start.2 = ((bf16[8,144,512]{2,1,0:T(8,128)(2,1)}), bf16[8,144,512]{2,1,0:T(8,128)(2,1)S(1)}, u32[]{:S(2)}, u32[]{:S(2)}) async-start(bf16[8,144,512]{2,1,0:T(8,128)(2,1)} %shard_map.102), calls=%async_computation.2 | async-start | bytes 2359296 | tf_op jit(solution)/shard_map/all_to_all | solution.py:243
  122.2 3.6 %copy-start.1 = (bf16[8,144,512]{2,1,0:T(8,128)(2,1)}, bf16[8,144,512]{2,1,0:T(8,128)(2,1)S(1)}, u32[]{:S(2)}) copy-start(bf16[8,144,512]{2,1,0:T(8,128)(2,1)S(1)} %all-to-all-done.2.refs_0_.refs_1_) | copy-start | bytes 3538948
  122.2 15.5 %all-to-all-start.3 = ((bf16[8,192,128]{2,1,0:T(8,128)(2,1)}), bf16[8,192,128]{2,1,0:T(8,128)(2,1)S(1)}, u32[]{:S(2)}, u32[]{:S(2)}) async-start(bf16[8,192,128]{2,1,0:T(8,128)(2,1)} %shard_map.103), calls=%async_computation.3 | async-start | bytes 786432 | tf_op jit(solution)/shard_map/all_to_all | solution.py:243
  142.2 3.4 %collective-permute-start = (bf16[384,1024]{1,0:T(8,128)(2,1)}, bf16[384,1024]{1,0:T(8,128)(2,1)S(1)}, u32[]{:S(2)}, u32[]{:S(2)}) collective-permute-start(bf16[384,1024]{1,0:T(8,128)(2,1)} %shard_map.106), channel_id=1, source_target_pairs={{0,1},{1,0},{2,3},{3,2},{4,5},{5,4},{6,7},{7,6},{8,9},{9,8},{10,11... | collective-permute-start | bytes 2359304 | tf_op jit(solution)/shard_map/ppermute | solution.py:284
  150.5 5.4 %collective-permute-start.1 = (bf16[384,1024]{1,0:T(8,128)(2,1)}, bf16[384,1024]{1,0:T(8,128)(2,1)S(1)}, u32[]{:S(2)}, u32[]{:S(2)}) collective-permute-start(bf16[384,1024]{1,0:T(8,128)(2,1)} %shard_map.108), channel_id=1, source_target_pairs={{0,1},{1,0},{2,3},{3,2},{4,5},{5,4},{6,7},{7,6},{8,9},{9,8},{10,11... | collective-permute-start | bytes 2359304 | tf_op jit(solution)/shard_map/ppermute | solution.py:284
  151.0 19.5 %collective-permute-start.2 = (bf16[384,1024]{1,0:T(8,128)(2,1)S(1)}, bf16[384,1024]{1,0:T(8,128)(2,1)S(1)}, u32[]{:S(2)}, u32[]{:S(2)}) collective-permute-start(bf16[384,1024]{1,0:T(8,128)(2,1)S(1)} %add_convert_fusion.1), channel_id=1, source_target_pairs={{0,2},{1,3},{2,0},{3,1},{4,6},{5,7},{6,4},{7,5},{8,10},{9,11},{10,... | collective-permute-start | bytes 2359304 | tf_op jit(solution)/shard_map/ppermute | solution.py:290

commit v5 on v4

--- a/solution.py
+++ b/solution.py
@@ -251,7 +251,7 @@
 
 def project(attended, retrieved, out_weight, cross_weight, block, width):
     rows, features = attended.shape
-    tiles = 2
+    tiles = 4
     tile = width // tiles
     left = pl.BlockSpec((rows, features), lambda t, b: (0, 0))
     right = pl.BlockSpec((features, tile), lambda t, b: (0, b[0] * tiles + t))

time: 174 us -> 177 us (1.017)
  Pallas kernels: 63.1 us -> 67.5 us
    pallas_call x4, Pallas kernels: 13.6 us -> 18 us  [project(): pl.pallas_call(project_kernel, grid_spec=pltpu.PrefetchScalarGridSpec(num...]
where the time goes in v5:
time: 177 us; the launch traced here: 176 us
  waiting for transfers between devices  79.8 us (45%)
  Pallas kernels  67.5 us (38%)
  starting transfers between devices  20.2 us (11%)
  local copies, waits for them, and re-layouts  4.42 us (2%)
  other arithmetic  4.19 us (2%)
    all_to_all x4, waiting for transfers between devices, exchange(): return lax.all_to_all(value, 'seq', split_axis=0, concat_axis=0, tiled=True)  66.4 us
    pallas_call x1, Pallas kernels, answer(): pl.pallas_call(functools.partial(answer_kernel, capacity), grid_spec=pltp...  19.2 us
    all_to_all x4, starting transfers between devices, exchange(): return lax.all_to_all(value, 'seq', split_axis=0, concat_axis=0, tiled=True)  18.2 us
    pallas_call x4, Pallas kernels, project(): pl.pallas_call(project_kernel, grid_spec=pltpu.PrefetchScalarGridSpec(num...  18 us
    pallas_call x1, Pallas kernels, attend(): pl.pallas_call(functools.partial(attend_kernel, rows), grid_spec=pltpu.Pr...  16.9 us
    ppermute x1, waiting for transfers between devices, project_and_sum(): lax.ppermute(total, 'mp', [(i, i ^ 2 * step) for i in range(groups)])  13.5 us
    pallas_call x1, Pallas kernels, combine(): pl.pallas_call(functools.partial(combine_kernel, picks, capacity), grid_s...  6.15 us
    pallas_call x1, Pallas kernels, pack_heads(): pl.pallas_call(pack_heads_kernel, grid=(devices,), out_shape=jax.ShapeDty...  5.56 us
  transfers between devices with their start and end apart: 7, of which 5 were waited for; matrix products, arithmetic and copies ran while one was open for 0% of the time, Pallas kernels for 32%

profile of v5, /device:TPU:0, one launch (start us, length us, event | category | flops | bytes accessed | tf_op | source)
XLA Modules:
  0.0 176.2 jit_solution(17602770437956943142)
XLA Ops:
  1.0 0.8 copy.18
  2.0 1.0 copy-done
  3.0 1.7 shard_map.100
  4.7 7.3 %all-to-all-start = ((bf16[8,144,512]{2,1,0:T(8,128)(2,1)}), bf16[8,144,512]{2,1,0:T(8,128)(2,1)S(1)}, u32[]{:S(2)}, u32[]{:S(2)}) async-start(bf16[8,144,512]{2,1,0:T(8,128)(2,1)} %shard_map.100), calls=%async_computation | async-start | bytes 2359296 | tf_op jit(solution)/shard_map/all_to_all | solution.py:243
  12.0 5.6 %shard_map.101 = bf16[8,960,128]{2,1,0:T(8,128)(2,1)} custom-call(bf16[384,512]{1,0:T(8,128)(2,1)} %q_ref.1, bf16[384,512]{1,0:T(8,128)(2,1)} %k_ref.1, bf16[384,512]{1,0:T(8,128)(2,1)} %v_ref.1), custom_call_target="tpu_custom_call" | custom-call | tf_op jit(solution)/shard_map/pallas_call | solution.py:34
  17.6 23.0 %all-to-all-done.asked_ref = bf16[8,144,512]{2,1,0:T(8,128)(2,1)S(1)} async-done(((bf16[8,144,512]{2,1,0:T(8,128)(2,1)}), bf16[8,144,512]{2,1,0:T(8,128)(2,1)S(1)}, u32[]{:S(2)}, u32[]{:S(2)}) %all-to-all-start) | async-done | bytes 1179680 | tf_op jit(solution)/shard_map/all_to_all | solution.py:243
  40.6 3.6 %all-to-all-start.1 = ((bf16[8,960,128]{2,1,0:T(8,128)(2,1)}), bf16[8,960,128]{2,1,0:T(8,128)(2,1)S(1)}, u32[]{:S(2)}, u32[]{:S(2)}) async-start(bf16[8,960,128]{2,1,0:T(8,128)(2,1)} %shard_map.101), calls=%async_computation.1 | async-start | bytes 3932160 | tf_op jit(solution)/shard_map/all_to_all | solution.py:243
  44.9 19.2 %shard_map.102 = bf16[8,144,512]{2,1,0:T(8,128)(2,1)} custom-call(s32[16]{0:T(128)} %reshape.84.want_ref, bf16[8,144,512]{2,1,0:T(8,128)(2,1)} %copy-done.2, bf16[8,128,512]{2,1,0:T(8,128)(2,1)} %refs_1_.1, bf16[8,128,512]{2,1,0:T(8,128)(2,1)} %refs_1_.1, bf16[8,128,512]{2,1,0:T(8,128)(2,1)} %refs_3_.1, bf16[8,128,512]{2,1,0:T(8,128)(2,1)} %refs_3_.1), custom_call_target="tpu_custom_call" | custom-call | tf_op jit(solution)/shard_map/pallas_call | solution.py:183
  64.0 25.8 %all-to-all-done.1.data_ref = bf16[8,960,128]{2,1,0:T(8,128)(2,1)S(1)} async-done(((bf16[8,960,128]{2,1,0:T(8,128)(2,1)}), bf16[8,960,128]{2,1,0:T(8,128)(2,1)S(1)}, u32[]{:S(2)}, u32[]{:S(2)}) %all-to-all-start.1) | async-done | bytes 1966112 | tf_op jit(solution)/shard_map/all_to_all | solution.py:243
  89.8 3.6 %all-to-all-start.2 = ((bf16[8,144,512]{2,1,0:T(8,128)(2,1)}), bf16[8,144,512]{2,1,0:T(8,128)(2,1)S(1)}, u32[]{:S(2)}, u32[]{:S(2)}) async-start(bf16[8,144,512]{2,1,0:T(8,128)(2,1)} %shard_map.102), calls=%async_computation.2 | async-start | bytes 2359296 | tf_op jit(solution)/shard_map/all_to_all | solution.py:243
  93.5 16.9 %shard_map.103 = bf16[8,192,128]{2,1,0:T(8,128)(2,1)} custom-call(s32[1]{0:T(128)} %bitcast.2.rep_ref, bf16[8,960,128]{2,1,0:T(8,128)(2,1)S(1)} %all-to-all-done.1.data_ref), custom_call_target="tpu_custom_call" | custom-call | tf_op jit(solution)/shard_map/pallas_call | solution.py:91
  110.4 11.8 %all-to-all-done.2.refs_0_.refs_1_ = bf16[8,144,512]{2,1,0:T(8,128)(2,1)S(1)} async-done(((bf16[8,144,512]{2,1,0:T(8,128)(2,1)}), bf16[8,144,512]{2,1,0:T(8,128)(2,1)S(1)}, u32[]{:S(2)}, u32[]{:S(2)}) %all-to-all-start.2) | async-done | bytes 1179680 | tf_op jit(solution)/shard_map/all_to_all | solution.py:243
  122.2 3.6 %all-to-all-start.3 = ((bf16[8,192,128]{2,1,0:T(8,128)(2,1)}), bf16[8,192,128]{2,1,0:T(8,128)(2,1)S(1)}, u32[]{:S(2)}, u32[]{:S(2)}) async-start(bf16[8,192,128]{2,1,0:T(8,128)(2,1)} %shard_map.103), calls=%async_computation.3 | async-start | bytes 786432 | tf_op jit(solution)/shard_map/all_to_all | solution.py:243
  125.9 6.1 %shard_map.104.ret_ref = bf16[384,512]{1,0:T(8,128)(2,1)} custom-call(s32[12]{0:T(128)} %copy-done.3, s32[12]{0:T(128)} %copy-done.4, bf16[8,144,512]{2,1,0:T(8,128)(2,1)} %copy-done.1, bf16[8,144,512]{2,1,0:T(8,128)(2,1)} %copy-done.1), custom_call_target="tpu_custom_call" | custom-call | tf_op jit(solution)/shard_map/pallas_call | solution.py:225
  132.0 5.7 %all-to-all-done.3 = bf16[8,192,128]{2,1,0:T(8,128)(2,1)S(1)} async-done(((bf16[8,192,128]{2,1,0:T(8,128)(2,1)}), bf16[8,192,128]{2,1,0:T(8,128)(2,1)S(1)}, u32[]{:S(2)}, u32[]{:S(2)}) %all-to-all-start.3) | async-done | bytes 393248 | tf_op jit(solution)/shard_map/all_to_all | solution.py:243
  138.0 0.8 copy.22
  138.9 4.5 %shard_map.106 = bf16[384,1024]{1,0:T(8,128)(2,1)} custom-call(s32[1]{0:T(128)} %bitcast.5.block_ref, bf16[384,512]{1,0:T(8,128)(2,1)} %bitcast.12, bf16[384,512]{1,0:T(8,128)(2,1)} %shard_map.104.ret_ref, bf16[512,4096]{1,0:T(8,128)(2,1)} %out_weight_ref.7, bf16[512,4096]{1,0:T(8,128)(2,1)} %cross_weight_ref.7), custom_call_target="tpu_custom_call" | custom-call | flops 805306368 | bytes 3670016 | tf_op jit(solution)/shard_map/pallas_call | solution.py:258
  143.3 4.5 %shard_map.105 = bf16[384,1024]{1,0:T(8,128)(2,1)} custom-call(s32[1]{0:T(128)} %bitcast.1.block_ref, bf16[384,512]{1,0:T(8,128)(2,1)} %bitcast.13, bf16[384,512]{1,0:T(8,128)(2,1)} %shard_map.104.ret_ref, bf16[512,4096]{1,0:T(8,128)(2,1)} %out_weight_ref.7, bf16[512,4096]{1,0:T(8,128)(2,1)} %cross_weight_ref.7), custom_call_target="tpu_custom_call" | custom-call | flops 805306368 | bytes 3670016 | tf_op jit(solution)/shard_map/pallas_call | solution.py:258
  147.9 1.4 add_convert_fusion.1
  149.3 4.5 %shard_map.108 = bf16[384,1024]{1,0:T(8,128)(2,1)} custom-call(s32[1]{0:T(128)} %bitcast.6.block_ref, bf16[384,512]{1,0:T(8,128)(2,1)} %bitcast.14, bf16[384,512]{1,0:T(8,128)(2,1)} %shard_map.104.ret_ref, bf16[512,4096]{1,0:T(8,128)(2,1)} %out_weight_ref.7, bf16[512,4096]{1,0:T(8,128)(2,1)} %cross_weight_ref.7), custom_call_target="tpu_custom_call" | custom-call | flops 805306368 | bytes 3670016 | tf_op jit(solution)/shard_map/pallas_call | solution.py:258
  154.3 1.5 collective-permute-start.2
  155.8 4.5 %shard_map.107 = bf16[384,1024]{1,0:T(8,128)(2,1)} custom-call(s32[1]{0:T(128)} %bitcast.block_ref, bf16[384,512]{1,0:T(8,128)(2,1)} %bitcast.15, bf16[384,512]{1,0:T(8,128)(2,1)} %shard_map.104.ret_ref, bf16[512,4096]{1,0:T(8,128)(2,1)} %out_weight_ref.7, bf16[512,4096]{1,0:T(8,128)(2,1)} %cross_weight_ref.7), custom_call_target="tpu_custom_call" | custom-call | flops 805306368 | bytes 3670016 | tf_op jit(solution)/shard_map/pallas_call | solution.py:258
  160.3 13.5 %collective-permute-done.2 = bf16[384,1024]{1,0:T(8,128)(2,1)S(1)} collective-permute-done((bf16[384,1024]{1,0:T(8,128)(2,1)S(1)}, bf16[384,1024]{1,0:T(8,128)(2,1)S(1)}, u32[]{:S(2)}, u32[]{:S(2)}) %collective-permute-start.2) | collective-permute-done | bytes 786464 | tf_op jit(solution)/shard_map/ppermute | solution.py:290
  173.7 2.4 %add_convert_fusion = bf16[384,1024]{1,0:T(8,128)(2,1)} fusion(bf16[384,1024]{1,0:T(8,128)(2,1)S(1)} %collective-permute-done.2, bf16[384,1024]{1,0:T(8,128)(2,1)S(1)} %collective-permute-done.1, bf16[384,1024]{1,0:T(8,128)(2,1)} %shard_map.107), kind=kLoop, calls=%fused_computation | loop fusion | flops 2359296 | bytes 3145728 | tf_op jit(solution)/shard_map/convert_element_type | solution.py:294
  (22 shorter events, 2.7 us)
Async XLA Ops:
  0.8 3.9 %copy-start.3 = (s32[12]{0:T(128)}, s32[12]{0:T(128)S(1)}, u32[]{:S(2)}) copy-start(s32[12]{0:T(128)S(1)} %reshape.78.owner_ref) | copy-start | bytes 148
  1.0 3.7 %copy-start.4 = (s32[12]{0:T(128)}, s32[12]{0:T(128)S(1)}, u32[]{:S(2)}) copy-start(s32[12]{0:T(128)S(1)} %convert_reduce_fusion.rank_ref) | copy-start | bytes 148
  2.0 1.0 copy-start
  4.7 35.9 %all-to-all-start = ((bf16[8,144,512]{2,1,0:T(8,128)(2,1)}), bf16[8,144,512]{2,1,0:T(8,128)(2,1)S(1)}, u32[]{:S(2)}, u32[]{:S(2)}) async-start(bf16[8,144,512]{2,1,0:T(8,128)(2,1)} %shard_map.100), calls=%async_computation | async-start | bytes 2359296 | tf_op jit(solution)/shard_map/all_to_all | solution.py:243
  40.6 3.6 %copy-start.2 = (bf16[8,144,512]{2,1,0:T(8,128)(2,1)}, bf16[8,144,512]{2,1,0:T(8,128)(2,1)S(1)}, u32[]{:S(2)}) copy-start(bf16[8,144,512]{2,1,0:T(8,128)(2,1)S(1)} %all-to-all-done.asked_ref) | copy-start | bytes 3538948
  40.6 49.2 %all-to-all-start.1 = ((bf16[8,960,128]{2,1,0:T(8,128)(2,1)}), bf16[8,960,128]{2,1,0:T(8,128)(2,1)S(1)}, u32[]{:S(2)}, u32[]{:S(2)}) async-start(bf16[8,960,128]{2,1,0:T(8,128)(2,1)} %shard_map.101), calls=%async_computation.1 | async-start | bytes 3932160 | tf_op jit(solution)/shard_map/all_to_all | solution.py:243
  89.8 32.4 %all-to-all-start.2 = ((bf16[8,144,512]{2,1,0:T(8,128)(2,1)}), bf16[8,144,512]{2,1,0:T(8,128)(2,1)S(1)}, u32[]{:S(2)}, u32[]{:S(2)}) async-start(bf16[8,144,512]{2,1,0:T(8,128)(2,1)} %shard_map.102), calls=%async_computation.2 | async-start | bytes 2359296 | tf_op jit(solution)/shard_map/all_to_all | solution.py:243
  122.2 3.6 %copy-start.1 = (bf16[8,144,512]{2,1,0:T(8,128)(2,1)}, bf16[8,144,512]{2,1,0:T(8,128)(2,1)S(1)}, u32[]{:S(2)}) copy-start(bf16[8,144,512]{2,1,0:T(8,128)(2,1)S(1)} %all-to-all-done.2.refs_0_.refs_1_) | copy-start | bytes 3538948
  122.2 15.5 %all-to-all-start.3 = ((bf16[8,192,128]{2,1,0:T(8,128)(2,1)}), bf16[8,192,128]{2,1,0:T(8,128)(2,1)S(1)}, u32[]{:S(2)}, u32[]{:S(2)}) async-start(bf16[8,192,128]{2,1,0:T(8,128)(2,1)} %shard_map.103), calls=%async_computation.3 | async-start | bytes 786432 | tf_op jit(solution)/shard_map/all_to_all | solution.py:243
  143.3 4.5 %collective-permute-start = (bf16[384,1024]{1,0:T(8,128)(2,1)}, bf16[384,1024]{1,0:T(8,128)(2,1)S(1)}, u32[]{:S(2)}, u32[]{:S(2)}) collective-permute-start(bf16[384,1024]{1,0:T(8,128)(2,1)} %shard_map.106), channel_id=1, source_target_pairs={{0,1},{1,0},{2,3},{3,2},{4,5},{5,4},{6,7},{7,6},{8,9},{9,8},{10,11... | collective-permute-start | bytes 2359304 | tf_op jit(solution)/shard_map/ppermute | solution.py:284
  153.8 6.5 %collective-permute-start.1 = (bf16[384,1024]{1,0:T(8,128)(2,1)}, bf16[384,1024]{1,0:T(8,128)(2,1)S(1)}, u32[]{:S(2)}, u32[]{:S(2)}) collective-permute-start(bf16[384,1024]{1,0:T(8,128)(2,1)} %shard_map.108), channel_id=1, source_target_pairs={{0,1},{1,0},{2,3},{3,2},{4,5},{5,4},{6,7},{7,6},{8,9},{9,8},{10,11... | collective-permute-start | bytes 2359304 | tf_op jit(solution)/shard_map/ppermute | solution.py:284
  154.3 19.5 %collective-permute-start.2 = (bf16[384,1024]{1,0:T(8,128)(2,1)S(1)}, bf16[384,1024]{1,0:T(8,128)(2,1)S(1)}, u32[]{:S(2)}, u32[]{:S(2)}) collective-permute-start(bf16[384,1024]{1,0:T(8,128)(2,1)S(1)} %add_convert_fusion.1), channel_id=1, source_target_pairs={{0,2},{1,3},{2,0},{3,1},{4,6},{5,7},{6,4},{7,5},{8,10},{9,11},{10,... | collective-permute-start | bytes 2359304 | tf_op jit(solution)/shard_map/ppermute | solution.py:290
